TPU v7x, 32 devices: a whole 2x2x4 slice. The times are simulated.
32 devices in a mesh: dp: 8 (over y, x, core), mp: 4 (over z).
Axes of the slice: x: 2, y: 2, z: 4, core: 2. Of those that a mesh axis runs over, the one named last changes fastest.
Arguments:
- view_one: bfloat16 [1024, 4096], P('dp', 'mp'), may hold values from -400 to 400
- view_two: bfloat16 [1024, 4096], P('dp', 'mp'), may hold values from -400 to 400
- proj_weight: bfloat16 [4096, 4096], P(None, 'mp'), may hold values from -0.09375 to 0.09375
Outputs:
- grad_one: bfloat16 [1024, 4096], P('dp', 'mp')
- grad_two: bfloat16 [1024, 4096], P('dp', 'mp')
All inputs are finite; a program needn't handle non-finite values.
Results may differ from a plain program's by a relative error of at most 0.025.
Values may be sent and summed in bfloat16 or wider, within the bound.
A program may use at most 128 MiB of HBM per device.

v0:
```python
import jax
import jax.numpy as jnp
from jax import lax
from jax.sharding import PartitionSpec as P

OFF_WEIGHT = 0.0125
EPSILON = 1e-05


def contract_rows(left, right):
    return lax.dot_general(
        left, right, (((0,), (0,)), ((), ())), preferred_element_type=jnp.float32
    )


def times_transposed(left, right):
    return lax.dot_general(
        left, right, (((1,), (1,)), ((), ())), preferred_element_type=jnp.float32
    )


def local(view_one, view_two, proj_weight):
    row_count, local_width = view_one.shape
    batch_devices = lax.axis_size("dp")
    total_rows = row_count * batch_devices
    first = view_one.astype(jnp.float32)
    second = view_two.astype(jnp.float32)
    sum_one, sum_two = lax.psum((jnp.sum(first, axis=0), jnp.sum(second, axis=0)), "dp")
    center_one = sum_one / total_rows
    center_two = sum_two / total_rows
    centered_one = first - center_one
    centered_two = second - center_two
    square_one, square_two = lax.psum(
        (
            jnp.sum(centered_one * centered_one, axis=0),
            jnp.sum(centered_two * centered_two, axis=0),
        ),
        "dp",
    )
    variance_one = square_one / total_rows
    variance_two = square_two / total_rows
    inverse_one = lax.rsqrt(variance_one + EPSILON)
    inverse_two = lax.rsqrt(variance_two + EPSILON)
    norm_one = (centered_one * inverse_one).astype(jnp.bfloat16)
    norm_two = (centered_two * inverse_two).astype(jnp.bfloat16)
    whole_two = lax.all_gather(norm_two, "mp", axis=1, tiled=True)
    total_width = whole_two.shape[1]
    block_index = lax.axis_index("mp")
    slab_index = lax.axis_index("dp")
    shard_cols = total_width // batch_devices
    corr_part = contract_rows(norm_one, whole_two)
    corr_shard = lax.psum_scatter(corr_part, "dp", scatter_dimension=1, tiled=True) / total_rows
    row_ids = block_index * local_width + lax.broadcasted_iota(
        jnp.int32, (local_width, shard_cols), 0
    )
    col_ids = slab_index * shard_cols + lax.broadcasted_iota(
        jnp.int32, (local_width, shard_cols), 1
    )
    grad_shard = jnp.where(
        row_ids == col_ids, -2.0 * (1.0 - corr_shard), 2.0 * OFF_WEIGHT * corr_shard
    ).astype(jnp.bfloat16)
    piece = lax.all_gather(grad_shard, "dp", axis=1, tiled=True)
    upper = times_transposed(whole_two, piece)
    fresh = jnp.dot(norm_one, piece, preferred_element_type=jnp.float32)
    up_two = lax.psum_scatter(
        fresh.astype(jnp.bfloat16), "mp", scatter_dimension=1, tiled=True
    ).astype(jnp.float32)
    normal_one = norm_one.astype(jnp.float32)
    normal_two = norm_two.astype(jnp.float32)
    mean_up_one, cross_one, mean_up_two, cross_two = lax.psum(
        (
            jnp.sum(upper, axis=0),
            jnp.sum(upper * normal_one, axis=0),
            jnp.sum(up_two, axis=0),
            jnp.sum(up_two * normal_two, axis=0),
        ),
        "dp",
    )
    delta_one = (
        inverse_one * (upper - mean_up_one / total_rows - normal_one * (cross_one / total_rows))
    ).astype(jnp.bfloat16)
    delta_two = (
        inverse_two * (up_two - mean_up_two / total_rows - normal_two * (cross_two / total_rows))
    ).astype(jnp.bfloat16)
    partial_one = times_transposed(delta_one, proj_weight)
    partial_two = times_transposed(delta_two, proj_weight)
    summed_one, summed_two = (
        lax.psum_scatter(
            partial_one.astype(jnp.bfloat16), "mp", scatter_dimension=1, tiled=True
        ).astype(jnp.float32),
        lax.psum_scatter(
            partial_two.astype(jnp.bfloat16), "mp", scatter_dimension=1, tiled=True
        ).astype(jnp.float32),
    )
    return (summed_one.astype(jnp.bfloat16), summed_two.astype(jnp.bfloat16))


def solution(mesh):
    placed = (P("dp", "mp"), P("dp", "mp"), P(None, "mp"))
    return jax.shard_map(
        local, mesh=mesh, in_specs=placed, out_specs=(P("dp", "mp"), P("dp", "mp")), check_vma=False
    )
```

profile of v0, /device:TPU:0, one launch (start us, length us, event | category | flops | bytes accessed | tf_op | source)
XLA Modules:
  0.0 377.4 jit_solution(16696728663640979777)
XLA Ops:
  7.2 1.0 convert_reduce_fusion.1
  8.2 1.0 convert_reduce_fusion.2
  9.2 15.5 %all-reduce.2 = (f32[1024]{0:T(1024)S(1)}, f32[1024]{0:T(1024)S(1)}) all-reduce(f32[1024]{0:T(1024)S(1)} %convert_reduce_fusion.1, f32[1024]{0:T(1024)S(1)} %convert_reduce_fusion.2), channel_id=1, replica_groups=mesh['dp'=8,'mp'=4] {'dp'}, use_global_device_ids=true, to_apply=%region_5.0 | all-reduce | flops 2048 | bytes 16384 | tf_op jit(solution)/shard_map/psum | solution.py:28
  24.7 1.0 fusion.6
  25.7 1.0 fusion.4
  26.8 12.1 %all-reduce.1 = (f32[1024]{0:T(1024)S(1)}, f32[1024]{0:T(1024)S(1)}) all-reduce(f32[1024]{0:T(1024)S(1)} %fusion.4, f32[1024]{0:T(1024)S(1)} %fusion.6), channel_id=1, replica_groups=mesh['dp'=8,'mp'=4] {'dp'}, use_global_device_ids=true, to_apply=%region_7.0 | all-reduce | flops 2048 | bytes 16384 | tf_op jit(solution)/shard_map/psum | solution.py:33
  38.9 1.7 fusion.5
  40.7 0.0 reduce-scatter.5.cloned.1.call-start
  40.7 27.4 %all-gather.3.cloned.1.call-done = bf16[128,4096]{1,0:T(8,128)(2,1)} async-done(((bf16[128,1024]{1,0:T(8,128)(2,1)}), bf16[128,4096]{1,0:T(8,128)(2,1)}) %all-gather.3.cloned.1.call-update) | async-done | bytes 1048592 | tf_op jit(solution)/shard_map/all_gather | solution.py:46
  68.1 9.4 %fusion.26 = f32[1024,4096]{1,0:T(8,128)} fusion(bf16[128,4096]{1,0:T(8,128)(2,1)} %all-gather.3.cloned.1.call-done, bf16[128,1024]{1,0:T(8,128)(2,1)} %param.3, f32[1024]{0:T(1024)S(1)} %add_rsqrt_fusion.1, f32[1024]{0:T(1024)S(1)} %get-tuple-element.16), kind=kOutput, calls=%fused_computation.36 | convolution fusion | flops 1074266112 | bytes 18096128 | tf_op jit(solution)/shard_map/dot_general | solution.py:11
  77.5 0.0 all-gather.5.cloned.1.call-start
  77.6 115.5 %reduce-scatter.5.cloned.1.call-done = f32[1024,512]{1,0:T(8,128)} async-done(((f32[1024,4096]{1,0:T(8,128)}), f32[1024,512]{1,0:T(8,128)}) %reduce-scatter.5.cloned.1.call-update) | async-done | bytes 2097168 | tf_op jit(solution)/shard_map/reduce_scatter | solution.py:52
  193.1 3.1 select_convert_fusion
  196.3 56.0 %all-gather.5.cloned.1.call-done = bf16[1024,4096]{1,0:T(8,128)(2,1)} async-done(((bf16[1024,512]{1,0:T(8,128)(2,1)}), bf16[1024,4096]{1,0:T(8,128)(2,1)}) %all-gather.5.cloned.1.call-update) | async-done | bytes 8388624 | tf_op jit(solution)/shard_map/all_gather | solution.py:62
  252.4 5.7 %convolution_convert_fusion.1 = bf16[128,4096]{1,0:T(8,128)(2,1)} fusion(bf16[1024,4096]{1,0:T(8,128)(2,1)} %all-gather.5.cloned.1.call-done, bf16[128,1024]{1,0:T(8,128)(2,1)S(1)} %copy-done, f32[1024]{0:T(1024)S(1)} %add_rsqrt_fusion.1, f32[1024]{0:T(1024)S(1)} %get-tuple-element.16), kind=kOutput, calls=%fused_computation.1 | convolution fusion | flops 1074790400 | bytes 9707520 | tf_op jit(solution)/shard_map/dot_general | solution.py:64
  258.2 6.3 %fusion.28 = (f32[1024]{0:T(1024)S(1)}, f32[1024]{0:T(1024)S(1)}, f32[128,1024]{1,0:T(8,128)S(1)}) fusion(f32[1024]{0:T(1024)S(1)} %add_rsqrt_fusion.1, f32[1024]{0:T(1024)S(1)} %get-tuple-element.16, bf16[128,1024]{1,0:T(8,128)(2,1)S(1)} %copy-done, bf16[128,4096]{1,0:T(8,128)(2,1)S(1)} %copy-done.1, bf16[1024,4096]{1,0:T(8,128)(2,1)} %all-gather.5.cloned.1.call-done), kind=kOutput, calls=%fused_computation.47 | convolution fusion | flops 1074788352 | bytes 10240000 | tf_op jit(solution)/shard_map/dot_general | solution.py:17
  264.5 20.9 %reduce-scatter.9.cloned.1.call-done = bf16[128,1024]{1,0:T(8,128)(2,1)} async-done(((bf16[128,4096]{1,0:T(8,128)(2,1)}), bf16[128,1024]{1,0:T(8,128)(2,1)}) %reduce-scatter.9.cloned.1.call-update) | async-done | bytes 262160 | tf_op jit(solution)/shard_map/reduce_scatter | solution.py:65
  285.4 1.1 convert_reduce_fusion
  286.5 23.8 %all-reduce = (f32[1024]{0:T(1024)S(1)}, f32[1024]{0:T(1024)S(1)}, f32[1024]{0:T(1024)S(1)}, f32[1024]{0:T(1024)S(1)}) all-reduce(f32[1024]{0:T(1024)S(1)} %get-tuple-element.3, f32[1024]{0:T(1024)S(1)} %get-tuple-element.2, f32[1024]{0:T(1024)S(1)} %get-tuple-element.5, ...), channel_id=1, replica_groups=mesh['dp'=8,'mp'=4] {'dp'}, use_global_device_ids=true, to_apply=%region_12.13 | all-reduce | flops 4096 | bytes 32768 | tf_op jit(solution)/shard_map/psum | solution.py:70
  310.4 7.3 %convolution_convert_fusion = bf16[128,4096]{1,0:T(8,128)(2,1)} fusion(bf16[4096,1024]{1,0:T(8,128)(2,1)} %param.5, bf16[128,1024]{1,0:T(8,128)(2,1)S(1)} %copy-done.3, bf16[128,1024]{1,0:T(8,128)(2,1)} %reduce-scatter.9.cloned.1.call-done, f32[1024]{0:T(1024)S(1)} %broadcast_multiply_fusion, f32[1024]{0:T(1024)S(1)} %broadcast_multiply_fusion.1, ...), kind=kOutput, calls=%fused_computation | convolution fusion | flops 1075183616 | bytes 9973760 | tf_op jit(solution)/shard_map/dot_general | solution.py:17
  317.7 0.0 reduce-scatter.7.cloned.1.call-start
  317.8 7.4 %convolution_convert_fusion.2 = bf16[128,4096]{1,0:T(8,128)(2,1)} fusion(bf16[4096,1024]{1,0:T(8,128)(2,1)} %param.5, f32[128,1024]{1,0:T(8,128)S(1)} %get-tuple-element.14, f32[1024]{0:T(1024)S(1)} %broadcast_multiply_fusion.2, f32[1024]{0:T(1024)S(1)} %broadcast_multiply_fusion.3, f32[1024]{0:T(1024)S(1)} %add_rsqrt_fusion.1, ...), kind=kOutput, calls=%fused_computation.2 | convolution fusion | flops 1075576832 | bytes 10240000 | tf_op jit(solution)/shard_map/dot_general | solution.py:17
  325.2 16.9 %reduce-scatter.11.cloned.1.call-done = bf16[128,1024]{1,0:T(8,128)(2,1)} async-done(((bf16[128,4096]{1,0:T(8,128)(2,1)}), bf16[128,1024]{1,0:T(8,128)(2,1)}) %reduce-scatter.11.cloned.1.call-update) | async-done | bytes 262160 | tf_op jit(solution)/shard_map/reduce_scatter | solution.py:91
  342.1 28.5 %reduce-scatter.7.cloned.1.call-done = bf16[128,1024]{1,0:T(8,128)(2,1)} async-done(((bf16[128,4096]{1,0:T(8,128)(2,1)}), bf16[128,1024]{1,0:T(8,128)(2,1)}) %reduce-scatter.7.cloned.1.call-update) | async-done | bytes 262160 | tf_op jit(solution)/shard_map/reduce_scatter | solution.py:88
  (26 shorter events, 0.3 us)
Async XLA Ops:
  7.2 61.0 %all-gather.3.cloned.1.call-start = ((), (), s32[]{:S(2)}) async-start(), calls=%async_computation.4 | async-start | bytes 1310720 | tf_op jit(solution)/shard_map/all_gather | solution.py:46
  40.7 152.5 %reduce-scatter.5.cloned.1.call-start = ((), (), s32[]{:S(2)}) async-start(), calls=%async_computation.5 | async-start | bytes 18874368 | tf_op jit(solution)/shard_map/reduce_scatter | solution.py:52
  77.5 174.9 %copy-start = (bf16[128,1024]{1,0:T(8,128)(2,1)S(1)}, bf16[128,1024]{1,0:T(8,128)(2,1)}, u32[]{:S(2)}) copy-start(bf16[128,1024]{1,0:T(8,128)(2,1)} %param.3) | copy-start | bytes 786436
  77.5 174.8 %all-gather.5.cloned.1.call-start = ((), (), s32[]{:S(2)}) async-start(), calls=%async_computation.6 | async-start | bytes 9437184 | tf_op jit(solution)/shard_map/all_gather | solution.py:62
  196.3 61.9 %copy-start.1 = (bf16[128,4096]{1,0:T(8,128)(2,1)S(1)}, bf16[128,4096]{1,0:T(8,128)(2,1)}, u32[]{:S(2)}) copy-start(bf16[128,4096]{1,0:T(8,128)(2,1)} %all-gather.3.cloned.1.call-done) | copy-start | bytes 3145732
  196.3 89.1 %reduce-scatter.9.cloned.1.call-start = ((), (), s32[]{:S(2)}) async-start(), calls=%async_computation.8 | async-start | bytes 1310720 | tf_op jit(solution)/shard_map/reduce_scatter | solution.py:65
  258.1 27.3 %copy-start.2 = (bf16[128,1024]{1,0:T(8,128)(2,1)S(1)}, bf16[128,1024]{1,0:T(8,128)(2,1)}, u32[]{:S(2)}) copy-start(bf16[128,1024]{1,0:T(8,128)(2,1)} %param.4) | copy-start | bytes 786436
  258.1 52.3 %copy-start.3 = (bf16[128,1024]{1,0:T(8,128)(2,1)S(1)}, bf16[128,1024]{1,0:T(8,128)(2,1)}, u32[]{:S(2)}) copy-start(bf16[128,1024]{1,0:T(8,128)(2,1)} %fusion.5) | copy-start | bytes 786436
  258.1 83.9 %reduce-scatter.11.cloned.1.call-start = ((), (), s32[]{:S(2)}) async-start(), calls=%async_computation.9 | async-start | bytes 1310720 | tf_op jit(solution)/shard_map/reduce_scatter | solution.py:91
  317.7 52.9 %reduce-scatter.7.cloned.1.call-start = ((), (), s32[]{:S(2)}) async-start(), calls=%async_computation.7 | async-start | bytes 1310720 | tf_op jit(solution)/shard_map/reduce_scatter | solution.py:88
Sparse Core Ops, SparseCore 0:
  40.8 27.2 all-gather.2
  77.7 115.4 reduce-scatter.4
  196.4 55.9 all-gather.4
  258.3 27.1 reduce-scatter.8
  317.8 24.1 reduce-scatter.10
  344.8 25.7 reduce-scatter.6
where the time goes:
time: 378 us; the launch traced here: 377 us
  waiting for transfers between devices  265 us (70%)
  blocking collectives  51.4 us (14%)
  matrix products  36.2 us (10%)
  between operations  14.2 us (4%)
  other arithmetic  10.1 us (3%)
    reduce_scatter x1, waiting for transfers between devices, local(): lax.psum_scatter(corr_part, 'dp', scatter_dimension=1, tiled=True)  116 us
    all_gather x1, waiting for transfers between devices, local(): piece = lax.all_gather(grad_shard, 'dp', axis=1, tiled=True)  56 us
    reduce_scatter x1, waiting for transfers between devices, local(): lax.psum_scatter(partial_one.astype(jnp.bfloat16), 'mp', scatter_dimensio...  28.5 us
    all_gather x1, waiting for transfers between devices, local(): whole_two = lax.all_gather(norm_two, 'mp', axis=1, tiled=True)  27.4 us
    psum x1, blocking collectives, local(): lax.psum((jnp.sum(upper, axis=0), jnp.sum(upper * normal_one, axis=0), jn...  23.8 us
    dot_general x3, matrix products, times_transposed(): lax.dot_general(left, right, (((1,), (1,)), ((), ())), preferred_element_...  21.1 us
    reduce_scatter x1, waiting for transfers between devices, local(): lax.psum_scatter(fresh.astype(jnp.bfloat16), 'mp', scatter_dimension=1, t...  20.9 us
    reduce_scatter x1, waiting for transfers between devices, local(): lax.psum_scatter(partial_two.astype(jnp.bfloat16), 'mp', scatter_dimensio...  16.9 us
  transfers between devices with their start and end apart: 6, of which 6 were waited for; matrix products, arithmetic and copies ran while one was open for 4% of the time, Pallas kernels for 0%

commit v1 on v0

--- a/solution.py
+++ b/solution.py
@@ -95,8 +95,47 @@
     return (summed_one.astype(jnp.bfloat16), summed_two.astype(jnp.bfloat16))
 
 
+def local_gram(view_one, view_two, proj_weight):
+    row_count, local_width = view_one.shape
+    total_rows = row_count * lax.axis_size("dp")
+    mine = lax.axis_index("dp") * row_count
+    views = lax.all_gather(jnp.stack([view_one, view_two]), "dp", axis=1, tiled=True)
+    values = views.astype(jnp.float32)
+    centered = values - jnp.mean(values, axis=1, keepdims=True)
+    inverse = lax.rsqrt(jnp.mean(centered * centered, axis=1, keepdims=True) + EPSILON)
+    norm = (centered * inverse).astype(jnp.bfloat16)
+    own = lax.dynamic_slice_in_dim(norm, mine, row_count, axis=1)
+    gram = lax.dot_general(
+        own, norm, (((2,), (2,)), ((0,), (0,))), preferred_element_type=jnp.float32
+    )
+    gram = lax.psum(gram.astype(jnp.bfloat16), "mp")
+    normal = norm.astype(jnp.float32)
+    diagonal = jnp.mean(normal[0] * normal[1], axis=0)
+    slope = 2.0 * (diagonal - 1.0) - 2.0 * OFF_WEIGHT * diagonal
+    up = lax.dot_general(
+        gram[::-1], norm, (((2,), (1,)), ((0,), (0,))), preferred_element_type=jnp.float32
+    )
+    own = own.astype(jnp.float32)
+    up = up * (2.0 * OFF_WEIGHT / total_rows) + own[::-1] * slope
+    mean_up, cross = lax.psum(
+        (jnp.sum(up, axis=1, keepdims=True), jnp.sum(up * own, axis=1, keepdims=True)), "dp"
+    )
+    delta = (inverse * (up - mean_up / total_rows - own * (cross / total_rows))).astype(jnp.bfloat16)
+    partial = lax.dot_general(
+        delta, proj_weight, (((2,), (1,)), ((), ())), preferred_element_type=jnp.float32
+    ).astype(jnp.bfloat16)
+    summed = lax.psum_scatter(partial, "mp", scatter_dimension=2, tiled=True)
+    return summed[0], summed[1]
+
+
 def solution(mesh):
     placed = (P("dp", "mp"), P("dp", "mp"), P(None, "mp"))
-    return jax.shard_map(
-        local, mesh=mesh, in_specs=placed, out_specs=(P("dp", "mp"), P("dp", "mp")), check_vma=False
-    )
+
+    def whole(view_one, view_two, proj_weight):
+        batch, features = view_one.shape
+        form = local_gram if 2 * batch <= features else local
+        return jax.shard_map(
+            form, mesh=mesh, in_specs=placed, out_specs=(P("dp", "mp"), P("dp", "mp")), check_vma=False
+        )(view_one, view_two, proj_weight)
+
+    return whole

time: 378 us -> 187 us (0.49)
  waiting for transfers between devices: 265 us -> 117 us
  blocking collectives: 51.4 us -> 23.3 us
  matrix products: 36.2 us -> 12.3 us
  other arithmetic: 10.1 us -> 15.2 us
  local copies, waits for them, and re-layouts: 0.01 us -> 4.95 us
    reduce_scatter x4 -> x1, waiting for transfers between devices: 182 us -> 42.2 us  [local_gram(): summed = lax.psum_scatter(partial, 'mp', scatter_dimension=2, tiled=True)]
    all_gather x2 -> x1, waiting for transfers between devices: 83.4 us -> 40.2 us  [local_gram(): lax.all_gather(jnp.stack([view_one, view_two]), 'dp', axis=1, tiled=True)]
    psum x0 -> x1, waiting for transfers between devices: none -> 34.4 us  [local_gram(): gram = lax.psum(gram.astype(jnp.bfloat16), 'mp')]
    psum x3 -> x1, blocking collectives: 51.4 us -> 23.3 us  [local_gram(): lax.psum((jnp.sum(up, axis=1, keepdims=True), jnp.sum(up * own, axis=1, k...]
    dot_general x5 -> x3, matrix products: 36.2 us -> 12.3 us  [the longest x1 7.31 us: local_gram(): lax.dot_general(delta, proj_weight, (((2,), (1,)), ((), ())), preferred_e...]
    reduce_sum x5 -> x3, other arithmetic: 5.17 us -> 8.28 us  [the longest x1 4 us: local_gram(): diagonal = jnp.mean(normal[0] * normal[1], axis=0)]
  transfers between devices with their start and end apart: 6 -> 3, of which waited for: 6 -> 3; matrix products, arithmetic and copies ran while one was open for 4% -> 2% of each run, Pallas kernels for 0% -> 0%
where the time goes in v1:
time: 187 us
  waiting for transfers between devices  117 us (63%)
  blocking collectives  23.3 us (12%)
  other arithmetic  15.2 us (8%)
  between operations  13.8 us (7%)
  matrix products  12.3 us (7%)
  local copies, waits for them, and re-layouts  4.95 us (3%)
    reduce_scatter x1, waiting for transfers between devices, local_gram(): summed = lax.psum_scatter(partial, 'mp', scatter_dimension=2, tiled=True)  42.2 us
    all_gather x1, waiting for transfers between devices, local_gram(): lax.all_gather(jnp.stack([view_one, view_two]), 'dp', axis=1, tiled=True)  40.2 us
    psum x1, waiting for transfers between devices, local_gram(): gram = lax.psum(gram.astype(jnp.bfloat16), 'mp')  34.4 us
    psum x1, blocking collectives, local_gram(): lax.psum((jnp.sum(up, axis=1, keepdims=True), jnp.sum(up * own, axis=1, k...  23.3 us
    dot_general x1, matrix products, local_gram(): lax.dot_general(delta, proj_weight, (((2,), (1,)), ((), ())), preferred_e...  7.31 us
    convert_element_type x1, other arithmetic, local_gram(): normal = norm.astype(jnp.float32)  4.9 us
    reduce_sum x1, other arithmetic, local_gram(): diagonal = jnp.mean(normal[0] * normal[1], axis=0)  4 us
  transfers between devices with their start and end apart: 3, of which 3 were waited for; matrix products, arithmetic and copies ran while one was open for 2% of the time, Pallas kernels for 0%

profile of v1, /device:TPU:0, one launch (start us, length us, event | category | flops | bytes accessed | tf_op | source)
XLA Modules:
  0.0 186.5 jit_solution(9058387585671960278)
XLA Ops:
  7.2 0.0 all-gather.2.cloned.1.call-start
  7.2 1.9 %pad_maximum_fusion = bf16[2,128,1024]{2,1,0:T(8,128)(2,1)} fusion(bf16[1,128,1024]{2,1,0:T(8,128)(2,1)} %bitcast.20, bf16[1,128,1024]{2,1,0:T(8,128)(2,1)} %bitcast.21), kind=kLoop, calls=%fused_computation.16 | loop fusion | flops 262144 | bytes 1048576 | tf_op jit(solution)/shard_map/stack | solution.py:102
  9.1 0.0 all-gather.2.cloned.1.call-update
  9.1 0.0 all-reduce.3.cloned.1.call-start
  9.2 40.2 %all-gather.2.cloned.1.call-done = bf16[2,1024,1024]{2,1,0:T(8,128)(2,1)} async-done(((bf16[2,128,1024]{2,1,0:T(8,128)(2,1)}), bf16[2,1024,1024]{2,1,0:T(8,128)(2,1)}) %all-gather.2.cloned.1.call-update) | async-done | bytes 4194320 | tf_op jit(solution)/shard_map/all_gather | solution.py:102
  49.4 3.2 %convert_reduce_fusion = f32[2,1024]{1,0:T(2,128)S(1)} fusion(bf16[2,1024,1024]{2,1,0:T(8,128)(2,1)} %all-gather.2.cloned.1.call-done), kind=kLoop, calls=%fused_computation.1 | loop fusion | flops 4192256 | bytes 4202496 | tf_op jit(solution)/shard_map/reduce_sum | solution.py:104
  52.6 0.2 copy-done.1
  52.8 1.1 fusion.2
  53.9 4.9 %fusion.20 = (f32[2,1024,1024]{2,1,0:T(8,128)}, bf16[2,1024,1024]{2,1,0:T(8,128)(2,1)S(1)}) fusion(f32[2,1024]{1,0:T(2,128)S(1)} %add_rsqrt_fusion, f32[2,1024]{1,0:T(2,128)S(1)} %broadcast_multiply_fusion, bf16[2,1024,1024]{2,1,0:T(8,128)(2,1)S(1)} %copy-done.1), kind=kLoop, calls=%fused_computation.34 | loop fusion | flops 10485760 | bytes 16793600 | tf_op jit(solution)/shard_map/convert_element_type | solution.py:112
  58.8 0.1 dynamic-slice_convert_fusion
  58.9 1.9 copy-done
  60.8 1.5 convolution_convert_fusion
  62.3 0.1 rev.7
  62.4 0.9 rev.6
  63.3 0.0 all-reduce.3.cloned.1.call-update
  63.4 0.0 reduce-scatter.2.cloned.1.call-start
  63.4 4.0 %fusion.9 = f32[1024]{0:T(1024)S(1)} fusion(f32[2,1024,1024]{2,1,0:T(8,128)} %get-tuple-element.6), kind=kLoop, calls=%fused_computation.10 | loop fusion | flops 2096128 | bytes 8392704 | tf_op jit(solution)/shard_map/reduce_sum | solution.py:113
  67.4 34.4 %all-reduce.3.cloned.1.call-done = bf16[2,128,1024]{2,1,0:T(8,128)(2,1)} async-done(((bf16[2,128,1024]{2,1,0:T(8,128)(2,1)}), bf16[2,128,1024]{2,1,0:T(8,128)(2,1)}) %all-reduce.3.cloned.1.call-update) | async-done | bytes 524304 | tf_op jit(solution)/shard_map/psum | solution.py:111
  101.8 3.5 %fusion.19 = (f32[2,1024]{1,0:T(2,128)S(1)}, f32[2,1024]{1,0:T(2,128)S(1)}, f32[2,128,1024]{2,1,0:T(8,128)S(1)}) fusion(bf16[2,1024,1024]{2,1,0:T(8,128)(2,1)} %copy-done, s32[]{:T(128)S(6)} %select_n.3, f32[2,128,1024]{2,1,0:T(8,128)S(1)} %rev.7, f32[1024]{0:T(1024)S(1)} %multiply_subtract_fusion, bf16[2,128,1024]{2,1,0:T(8,128)(2,1)} %all-reduce.3.cloned.1.call-done), kind=kOutput, calls=%fused_computation.33 | convolution fusion | flops 538701824 | bytes 7360516 | tf_op jit(solution)/shard_map/dot_general | solution.py:115
  105.3 23.3 %all-reduce = (f32[2,1,1024]{2,0,1:T(2,128)S(1)}, f32[2,1,1024]{2,0,1:T(2,128)S(1)}) all-reduce(f32[2,1,1024]{2,0,1:T(2,128)S(1)} %bitcast.23, f32[2,1,1024]{2,0,1:T(2,128)S(1)} %bitcast.22), channel_id=1, replica_groups=mesh['dp'=8,'mp'=4] {'dp'}, use_global_device_ids=true, to_apply=%region_7.0 | all-reduce | flops 4096 | bytes 32768 | tf_op jit(solution)/shard_map/psum | solution.py:120
  128.6 7.3 %fusion.6 = bf16[2,128,4096]{2,1,0:T(8,128)(2,1)} fusion(bf16[4096,1024]{1,0:T(8,128)(2,1)} %param.5, f32[2,128,1024]{2,1,0:T(8,128)S(1)} %get-tuple-element.10, f32[2,1024]{1,0:T(2,128)S(1)} %get-tuple-element.11, f32[2,1024]{1,0:T(2,128)S(1)} %get-tuple-element.12, f32[2,1024]{1,0:T(2,128)S(1)} %add_rsqrt_fusion, bf16[2,1024,1024]{2,1,0:T(8,128)(2,1)} %copy-done, ...), kind=kOutput, calls=%fused_computation.8 | convolution fusion | flops 2150105088 | bytes 12083204 | tf_op jit(solution)/shard_map/dot_general | solution.py:124
  135.9 0.0 reduce-scatter.2.cloned.1.call-update
  135.9 42.2 %reduce-scatter.2.cloned.1.call-done = bf16[2,128,1024]{2,1,0:T(8,128)(2,1)} async-done(((bf16[2,128,4096]{2,1,0:T(8,128)(2,1)}), bf16[2,128,1024]{2,1,0:T(8,128)(2,1)}) %reduce-scatter.2.cloned.1.call-update) | async-done | bytes 524304 | tf_op jit(solution)/shard_map/reduce_scatter | solution.py:127
  178.1 1.9 slice_bitcast_fusion
  (6 shorter events, 0.0 us)
Async XLA Ops:
  7.2 42.2 %all-gather.2.cloned.1.call-start = ((), (), s32[]{:S(2)}) async-start(), calls=%async_computation.1 | async-start | bytes 4718592 | tf_op jit(solution)/shard_map/all_gather | solution.py:102
  9.1 92.7 %all-reduce.3.cloned.1.call-start = ((), (), s32[]{:S(2)}) async-start(), calls=%async_computation.2 | async-start | bytes 1048576 | tf_op jit(solution)/shard_map/psum | solution.py:111
  49.4 3.4 %copy-start.1 = (bf16[2,1024,1024]{2,1,0:T(8,128)(2,1)S(1)}, bf16[2,1024,1024]{2,1,0:T(8,128)(2,1)}, u32[]{:S(2)}) copy-start(bf16[2,1024,1024]{2,1,0:T(8,128)(2,1)} %all-gather.2.cloned.1.call-done) | copy-start | bytes 12582916
  58.8 2.0 %copy-start = (bf16[2,1024,1024]{2,1,0:T(8,128)(2,1)}, bf16[2,1024,1024]{2,1,0:T(8,128)(2,1)S(1)}, u32[]{:S(2)}) copy-start(bf16[2,1024,1024]{2,1,0:T(8,128)(2,1)S(1)} %get-tuple-element.7) | copy-start | bytes 12582916
  63.4 114.8 %reduce-scatter.2.cloned.1.call-start = ((), (), s32[]{:S(2)}) async-start(), calls=%async_computation.3 | async-start | bytes 2621440 | tf_op jit(solution)/shard_map/reduce_scatter | solution.py:127
Sparse Core Ops, SparseCore 0:
  9.9 39.4 all-gather.1
  63.5 38.2 all-reduce.2
  136.1 42.0 reduce-scatter.1

commit v2 on v0

--- a/solution.py
+++ b/solution.py
@@ -1,10 +1,381 @@
 import jax
 import jax.numpy as jnp
 from jax import lax
+from jax.experimental import pallas as pl
+from jax.experimental.pallas import tpu as pltpu
 from jax.sharding import PartitionSpec as P
 
 OFF_WEIGHT = 0.0125
 EPSILON = 1e-05
+MESH = pl.DeviceIdType.MESH
+DP, MP = 8, 4
+PARTS = 4
+
+
+def times_t(left, right):
+    return lax.dot_general(
+        left, right, (((1,), (1,)), ((), ())), preferred_element_type=jnp.float32
+    )
+
+
+def fused(
+    one_ref, two_ref, weight_hbm, grad_one_ref, grad_two_ref,
+    weight, norm, stat, back, inverse_ref, diagonal, up, own_gram, from_end, from_mid, gram,
+    delta, part, from_outer, from_inner,
+    weight_sem, stat_s, stat_r, back_s, back_r, norm_s, norm_r,
+    gram_s, end_r, mid_r, total_s, total_r, part_s, outer_r, inner_r,
+):
+    rows, width = one_ref.shape
+    total_rows = rows * DP
+    bf16, f32 = jnp.bfloat16, jnp.float32
+    a, m = lax.axis_index("dp"), lax.axis_index("mp")
+    core, along_x, along_y = lax.rem(a, 2), lax.rem(lax.div(a, 2), 2), lax.div(a, 4)
+
+    def peer(r):
+        at = a
+        if r & 1:
+            at = at + 1 - 2 * core
+        if r & 2:
+            at = at + 2 - 4 * along_x
+        if r & 4:
+            at = at + 4 - 8 * along_y
+        return (at, m)
+
+    low = m < 2
+    is_mid = jnp.logical_and(m > 0, m < MP - 1)
+    is_end = jnp.logical_not(is_mid)
+    inner = (a, jnp.where(low, m + 1, m - 1))
+    outer = (a, jnp.where(low, jnp.maximum(m - 1, 0), jnp.minimum(m + 1, MP - 1)))
+
+    def remote(src, dst, send, recv, to):
+        return pltpu.make_async_remote_copy(
+            src_ref=src, dst_ref=dst, send_sem=send, recv_sem=recv, device_id=to, device_id_type=MESH
+        )
+
+    load = pltpu.make_async_copy(weight_hbm, weight, weight_sem)
+    load.start()
+
+    barrier = pltpu.get_barrier_semaphore()
+    for r in range(1, DP):
+        pl.semaphore_signal(barrier, inc=1, device_id=peer(r), device_id_type=MESH)
+    pl.semaphore_signal(barrier, inc=1, device_id=inner, device_id_type=MESH)
+
+    @pl.when(is_mid)
+    def _():
+        pl.semaphore_signal(barrier, inc=1, device_id=outer, device_id_type=MESH)
+
+    for v, ref in enumerate((one_ref, two_ref)):
+        x = ref[...].astype(f32)
+        mean = jnp.sum(x, axis=0, keepdims=True) / rows
+        x = x - mean
+        stat[0, pl.ds(2 * v, 1)] = mean
+        stat[0, pl.ds(2 * v + 1, 1)] = jnp.sum(x * x, axis=0, keepdims=True)
+
+    pl.semaphore_wait(barrier, DP + jnp.where(is_mid, 1, 0))
+
+    def stat_copy(r):
+        return remote(stat.at[0], stat.at[r], stat_s.at[r], stat_r.at[r], peer(r))
+
+    for r in range(DP - 1, 0, -1):
+        stat_copy(r).start()
+    for r in range(1, DP):
+        stat_copy(r).wait_recv()
+    for v, ref in enumerate((one_ref, two_ref)):
+        means = [stat[r, pl.ds(2 * v, 1)] for r in range(DP)]
+        mean = sum(means) / DP
+        square = sum(stat[r, pl.ds(2 * v + 1, 1)] for r in range(DP))
+        square = square + rows * sum((one - mean) * (one - mean) for one in means)
+        inverse = lax.rsqrt(square / total_rows + EPSILON)
+        inverse_ref[pl.ds(v, 1)] = inverse
+        norm[v, pl.ds(0, rows)] = ((ref[...].astype(f32) - mean) * inverse).astype(bf16)
+
+    def norm_copy(v, src, dst, via):
+        return remote(
+            norm.at[v, pl.ds(src * rows, rows)], norm.at[v, pl.ds(dst * rows, rows)],
+            norm_s.at[dst, v], norm_r.at[dst, v], peer(via),
+        )
+
+    def norm_wait(v, slot):
+        norm_copy(v, slot, slot, 1).wait_recv()
+
+    sent = []
+
+    def norm_send(v, src, dst, via):
+        copy = norm_copy(v, src, dst, via)
+        copy.start()
+        sent.append(copy)
+
+    norm_send(0, 0, 2, 2)
+    norm_send(1, 0, 4, 4)
+    norm_send(0, 0, 1, 1)
+    norm_send(1, 0, 1, 1)
+    norm_send(1, 0, 2, 2)
+    norm_send(0, 0, 4, 4)
+
+    chunks = ((0, 0), (1, 0), (0, 1), (1, 2), (1, 1), (0, 2), (0, 3), (1, 3))
+    wide = 2 * rows
+
+    def end_copy(k):
+        return remote(own_gram.at[k], from_end.at[k], gram_s.at[k], end_r.at[k], inner)
+
+    def mid_copy(k):
+        return remote(own_gram.at[k], from_mid.at[k], gram_s.at[k], mid_r.at[k], inner)
+
+    def total_copy(k):
+        return remote(gram.at[k], gram.at[k], total_s.at[k], total_r.at[k], outer)
+
+    def own(k):
+        v, p = chunks[k]
+        own_gram[k] = times_t(norm[v, pl.ds(0, rows)], norm[v, pl.ds(p * wide, wide)]).astype(bf16)
+
+        @pl.when(is_end)
+        def _():
+            end_copy(k).start()
+
+    def across(k):
+        @pl.when(is_mid)
+        def _():
+            end_copy(k).wait_recv()
+            own_gram[k] = (own_gram[k].astype(f32) + from_end[k].astype(f32)).astype(bf16)
+            mid_copy(k).start()
+
+    def back_out(k):
+        @pl.when(is_mid)
+        def _():
+            mid_copy(k).wait_recv()
+            gram[k] = (own_gram[k].astype(f32) + from_mid[k].astype(f32)).astype(bf16)
+            total_copy(k).start()
+
+    def use(k):
+        v, p = chunks[k]
+
+        @pl.when(is_end)
+        def _():
+            total_copy(k).wait_recv()
+
+        product = jnp.dot(gram[k], norm[1 - v, pl.ds(p * wide, wide)], preferred_element_type=f32)
+        if p == 0:
+            up[1 - v] = product
+        else:
+            up[1 - v] += product
+
+    def match(p):
+        both = norm[0, pl.ds(p * wide, wide)].astype(f32) * norm[1, pl.ds(p * wide, wide)].astype(f32)
+        both = jnp.sum(both, axis=0, keepdims=True)
+        diagonal[pl.ds(0, 1)] = both if p == 0 else diagonal[pl.ds(0, 1)] + both
+
+    norm_wait(0, 1)
+    own(0)
+    norm_wait(1, 1)
+    own(1)
+    across(0)
+    across(1)
+    match(0)
+    back_out(0)
+    back_out(1)
+
+    norm_wait(0, 2)
+    norm_send(0, 2, 6, 4)
+    norm_send(0, 2, 3, 1)
+    norm_wait(1, 4)
+    norm_send(1, 4, 6, 2)
+    norm_send(1, 4, 5, 1)
+    norm_wait(0, 3)
+    own(2)
+    norm_wait(1, 5)
+    own(3)
+    use(0)
+    use(1)
+    across(2)
+    across(3)
+    back_out(2)
+    back_out(3)
+
+    norm_wait(1, 2)
+    norm_send(1, 2, 3, 1)
+    norm_wait(0, 4)
+    norm_send(0, 4, 5, 1)
+    norm_wait(1, 3)
+    own(4)
+    norm_wait(0, 5)
+    own(5)
+    use(2)
+    use(3)
+    across(4)
+    across(5)
+    match(1)
+    match(2)
+    back_out(4)
+    back_out(5)
+
+    norm_wait(0, 6)
+    norm_send(0, 6, 7, 1)
+    norm_wait(1, 6)
+    norm_send(1, 6, 7, 1)
+    norm_wait(0, 7)
+    own(6)
+    norm_wait(1, 7)
+    own(7)
+    across(6)
+    across(7)
+    use(4)
+    use(5)
+    match(3)
+    back_out(6)
+    back_out(7)
+    use(6)
+    use(7)
+
+    diag = diagonal[pl.ds(0, 1)] / total_rows
+    slope = 2.0 * (diag - 1.0) - 2.0 * OFF_WEIGHT * diag
+    for v in range(2):
+        mine = norm[v, pl.ds(0, rows)].astype(f32)
+        other = norm[1 - v, pl.ds(0, rows)].astype(f32)
+        value = up[v] * (2.0 * OFF_WEIGHT / total_rows) + other * slope
+        up[v] = value
+        back[0, pl.ds(2 * v, 1)] = jnp.sum(value, axis=0, keepdims=True)
+        back[0, pl.ds(2 * v + 1, 1)] = jnp.sum(value * mine, axis=0, keepdims=True)
+
+    def back_copy(r):
+        return remote(back.at[0], back.at[r], back_s.at[r], back_r.at[r], peer(r))
+
+    for r in range(DP - 1, 0, -1):
+        back_copy(r).start()
+    for r in range(1, DP):
+        back_copy(r).wait_recv()
+    for v in range(2):
+        mean_up = sum(back[r, pl.ds(2 * v, 1)] for r in range(DP)) / total_rows
+        cross = sum(back[r, pl.ds(2 * v + 1, 1)] for r in range(DP)) / total_rows
+        mine = norm[v, pl.ds(0, rows)].astype(f32)
+        delta[pl.ds(v * rows, rows)] = (
+            inverse_ref[pl.ds(v, 1)] * (up[v] - mean_up - mine * cross)
+        ).astype(bf16)
+
+    load.wait()
+    slim = width // PARTS
+
+    def outward(j, c):
+        return remote(part.at[j, c], from_outer.at[j, c], part_s.at[j, c], outer_r.at[j, c], inner)
+
+    def over(j, c):
+        return remote(part.at[j, c], from_inner.at[3 - j, c], part_s.at[j, c], inner_r.at[3 - j, c], inner)
+
+    def homeward(c):
+        return remote(part.at[0, c], from_inner.at[0, c], part_s.at[0, c], inner_r.at[0, c], outer)
+
+    @pl.loop(0, MP * PARTS)
+    def _(step):
+        j = MP - 1 - lax.div(step, PARTS)
+        c = lax.rem(step, PARTS)
+        block = jnp.where(low, j, MP - 1 - j)
+        start = pl.multiple_of(block * width + c * slim, slim)
+        part[j, c] = times_t(delta[...], weight[pl.ds(start, slim)]).astype(bf16)
+
+        @pl.when(jnp.logical_and(is_end, j > 0))
+        def _():
+            outward(j, c).start()
+
+    def finish(c, value):
+        value = value.astype(bf16)
+        grad_one_ref[:, pl.ds(c * slim, slim)] = value[:rows]
+        grad_two_ref[:, pl.ds(c * slim, slim)] = value[rows:]
+
+    @pl.when(is_end)
+    def _():
+        for c in range(PARTS):
+            homeward(c).wait_recv()
+            finish(c, part[0, c].astype(f32) + from_inner[0, c].astype(f32))
+
+    @pl.when(is_mid)
+    def _():
+        def pass_on(j, c):
+            outward(j, c).wait_recv()
+            part[j, c] = (part[j, c].astype(f32) + from_outer[j, c].astype(f32)).astype(bf16)
+            over(j, c).start()
+
+        def pass_home(c):
+            over(3, c).wait_recv()
+            part[0, c] = (part[0, c].astype(f32) + from_inner[0, c].astype(f32)).astype(bf16)
+            homeward(c).start()
+
+        order = [(3, c) for c in range(PARTS)] + [(2, c) for c in range(PARTS)]
+        for at, (j, c) in enumerate(order):
+            pass_on(j, c)
+            if 1 <= at <= PARTS:
+                pass_home(at - 1)
+        for c in range(PARTS):
+            over(2, c).wait_recv()
+            outward(1, c).wait_recv()
+            finish(
+                c, part[1, c].astype(f32) + from_outer[1, c].astype(f32) + from_inner[1, c].astype(f32)
+            )
+
+    for r in range(1, DP):
+        stat_copy(r).wait_send()
+        back_copy(r).wait_send()
+    for copy in sent:
+        copy.wait_send()
+    for k in range(len(chunks)):
+        end_copy(k).wait_send()
+
+    @pl.when(is_mid)
+    def _():
+        for k in range(len(chunks)):
+            total_copy(k).wait_send()
+        for c in range(PARTS):
+            for j in (0, 2, 3):
+                outward(j, c).wait_send()
+
+    @pl.when(is_end)
+    def _():
+        for c in range(PARTS):
+            for j in (1, 2, 3):
+                outward(j, c).wait_send()
+
+
+def local_fused(view_one, view_two, proj_weight):
+    rows, width = view_one.shape
+    bf16, f32 = jnp.bfloat16, jnp.float32
+    dma = pltpu.SemaphoreType.DMA
+    slim = width // PARTS
+    out = jax.ShapeDtypeStruct((rows, width), bf16)
+    vmem = pl.BlockSpec(memory_space=pltpu.VMEM)
+    return pl.pallas_call(
+        fused,
+        out_shape=(out, out),
+        in_specs=[vmem, vmem, pl.BlockSpec(memory_space=pl.ANY)],
+        out_specs=(vmem, vmem),
+        scratch_shapes=[
+            pltpu.VMEM(proj_weight.shape, bf16),
+            pltpu.VMEM((2, DP * rows, width), bf16),
+            pltpu.VMEM((DP, 4, width), f32),
+            pltpu.VMEM((DP, 4, width), f32),
+            pltpu.VMEM((8, width), f32),
+            pltpu.VMEM((8, width), f32),
+            pltpu.VMEM((2, rows, width), f32),
+            pltpu.VMEM((8, rows, 2 * rows), bf16),
+            pltpu.VMEM((8, rows, 2 * rows), bf16),
+            pltpu.VMEM((8, rows, 2 * rows), bf16),
+            pltpu.VMEM((8, rows, 2 * rows), bf16),
+            pltpu.VMEM((2 * rows, width), bf16),
+            pltpu.VMEM((MP, PARTS, 2 * rows, slim), bf16),
+            pltpu.VMEM((MP, PARTS, 2 * rows, slim), bf16),
+            pltpu.VMEM((2, PARTS, 2 * rows, slim), bf16),
+            dma(()),
+            dma((DP,)), dma((DP,)), dma((DP,)), dma((DP,)),
+            dma((DP, 2)), dma((DP, 2)),
+            dma((8,)), dma((8,)), dma((8,)), dma((8,)), dma((8,)),
+            dma((MP, PARTS)), dma((MP, PARTS)), dma((2, PARTS)),
+        ],
+        compiler_params=pltpu.CompilerParams(
+            collective_id=0, has_side_effects=True, vmem_limit_bytes=48 * 1024 * 1024
+        ),
+        cost_estimate=pl.CostEstimate(
+            flops=4 * rows * width * (2 * DP * rows + MP * width),
+            bytes_accessed=2 * (MP * width * width + 4 * rows * width),
+            transcendentals=0,
+        ),
+    )(view_one, view_two, proj_weight)
 
 
 def contract_rows(left, right):
@@ -97,6 +468,14 @@
 
 def solution(mesh):
     placed = (P("dp", "mp"), P("dp", "mp"), P(None, "mp"))
-    return jax.shard_map(
-        local, mesh=mesh, in_specs=placed, out_specs=(P("dp", "mp"), P("dp", "mp")), check_vma=False
-    )
+
+    def whole(view_one, view_two, proj_weight):
+        batch, features = view_one.shape
+        suits = dict(mesh.shape) == {"dp": DP, "mp": MP}
+        suits = suits and batch % (DP * 128) == 0 and 2 * batch <= features and features <= 4096
+        return jax.shard_map(
+            local_fused if suits else local,
+            mesh=mesh, in_specs=placed, out_specs=(P("dp", "mp"), P("dp", "mp")), check_vma=False,
+        )(view_one, view_two, proj_weight)
+
+    return whole

time: 378 us -> 88.2 us (0.23)
  waiting for transfers between devices: 265 us -> 0 us
  Pallas kernels: 0 us -> 84.1 us
  blocking collectives: 51.4 us -> 0 us
  matrix products: 36.2 us -> 0 us
  between operations: 14.2 us -> 0.65 us
  other arithmetic: 10.1 us -> 0 us
    reduce_scatter x4 -> x0, waiting for transfers between devices: 182 us -> none  [the longest x1 116 us: local(): lax.psum_scatter(corr_part, 'dp', scatter_dimension=1, tiled=True)]
    pallas_call x0 -> x1, Pallas kernels: none -> 84.1 us  [local_fused(): pl.pallas_call(fused, out_shape=(out, out), in_specs=[vmem, vmem, pl.Bloc...]
    all_gather x2 -> x0, waiting for transfers between devices: 83.4 us -> none  [the longest x1 56 us: local(): piece = lax.all_gather(grad_shard, 'dp', axis=1, tiled=True)]
    psum x3 -> x0, blocking collectives: 51.4 us -> none  [the longest x1 23.8 us: local(): lax.psum((jnp.sum(upper, axis=0), jnp.sum(upper * normal_one, axis=0), jn...]
    dot_general x5 -> x0, matrix products: 36.2 us -> none  [the longest x3 21.1 us: times_transposed(): lax.dot_general(left, right, (((1,), (1,)), ((), ())), preferred_element_...]
    reduce_sum x5 -> x0, other arithmetic: 5.17 us -> none  [the longest x1 1.09 us: local(): jnp.sum(up_two, axis=0)]
    convert_element_type x2 -> x0, other arithmetic: 4.86 us -> none  [the longest x1 3.13 us: local(): grad_shard = jnp.where(row_ids == col_ids, -2.0 * (1.0 - corr_shard), 2.0...]
  transfers between devices with their start and end apart: 6 -> 0, of which waited for: 6 -> 0; matrix products, arithmetic and copies ran while one was open for 4% -> 0% of each run, Pallas kernels for 0% -> 0%
where the time goes in v2:
time: 88.2 us; the launch traced here: 88 us
  Pallas kernels  84.1 us (95%)
  local copies, waits for them, and re-layouts  3.3 us (4%)
    pallas_call x1, Pallas kernels, local_fused(): pl.pallas_call(fused, out_shape=(out, out), in_specs=[vmem, vmem, pl.Bloc...  84.1 us
    unnamed x6, local copies, waits for them, and re-layouts  3.3 us

profile of v2, /device:TPU:0, one launch (start us, length us, event | category | flops | bytes accessed | tf_op | source)
XLA Modules:
  0.0 88.0 jit_solution(2693649061915927701)
XLA Ops:
  0.6 0.0 copy-start
  0.6 0.9 %copy-done = bf16[128,1024]{1,0:T(8,128)(2,1)S(1)} copy-done((bf16[128,1024]{1,0:T(8,128)(2,1)S(1)}, bf16[128,1024]{1,0:T(8,128)(2,1)}, u32[]{:S(2)}) %copy-start) | copy-done | bytes 262168
  1.6 0.0 copy-start.1
  1.6 0.9 %copy-done.1 = bf16[128,1024]{1,0:T(8,128)(2,1)S(1)} copy-done((bf16[128,1024]{1,0:T(8,128)(2,1)S(1)}, bf16[128,1024]{1,0:T(8,128)(2,1)}, u32[]{:S(2)}) %copy-start.1) | copy-done | bytes 262168
  2.5 84.1 %shard_map.50 = (bf16[128,1024]{1,0:T(8,128)(2,1)S(1)}, bf16[128,1024]{1,0:T(8,128)(2,1)S(1)}) custom-call(bf16[128,1024]{1,0:T(8,128)(2,1)S(1)} %copy-done, bf16[128,1024]{1,0:T(8,128)(2,1)S(1)} %copy-done.1, bf16[4096,1024]{1,0:T(8,128)(2,1)} %weight_hbm.1), custom_call_target="tpu_custom_call" | custom-call | flops 3221225472 | bytes 9437184 | tf_op jit(solution)/shard_map/pallas_call | solution.py:343
  86.6 0.7 copy.7
  87.3 0.7 copy.8
Async XLA Ops:
  0.6 1.0 %copy-start = (bf16[128,1024]{1,0:T(8,128)(2,1)S(1)}, bf16[128,1024]{1,0:T(8,128)(2,1)}, u32[]{:S(2)}) copy-start(bf16[128,1024]{1,0:T(8,128)(2,1)} %one_ref.1) | copy-start | bytes 786436
  1.6 0.9 %copy-start.1 = (bf16[128,1024]{1,0:T(8,128)(2,1)S(1)}, bf16[128,1024]{1,0:T(8,128)(2,1)}, u32[]{:S(2)}) copy-start(bf16[128,1024]{1,0:T(8,128)(2,1)} %two_ref.1) | copy-start | bytes 786436

commit v3 on v2

--- a/solution.py
+++ b/solution.py
@@ -9,6 +9,7 @@
 EPSILON = 1e-05
 MESH = pl.DeviceIdType.MESH
 DP, MP = 8, 4
+AHEAD = 2
 PARTS = 4
 
 
@@ -19,13 +20,13 @@
 
 
 def fused(
-    one_ref, two_ref, weight_hbm, grad_one_ref, grad_two_ref,
-    weight, norm, stat, back, inverse_ref, diagonal, up, own_gram, from_end, from_mid, gram,
+    one_hbm, two_hbm, weight_hbm, grad_one_ref, grad_two_ref,
+    views, weight, norm, stat, back, inverse_ref, diagonal, up, own_gram, from_end, from_mid, gram,
     delta, part, from_outer, from_inner,
-    weight_sem, stat_s, stat_r, back_s, back_r, norm_s, norm_r,
+    view_sem, weight_sem, stat_s, stat_r, back_s, back_r, norm_s, norm_r,
     gram_s, end_r, mid_r, total_s, total_r, part_s, outer_r, inner_r,
 ):
-    rows, width = one_ref.shape
+    _, rows, width = views.shape
     total_rows = rows * DP
     bf16, f32 = jnp.bfloat16, jnp.float32
     a, m = lax.axis_index("dp"), lax.axis_index("mp")
@@ -52,6 +53,12 @@
             src_ref=src, dst_ref=dst, send_sem=send, recv_sem=recv, device_id=to, device_id_type=MESH
         )
 
+    fetch = [
+        pltpu.make_async_copy(ref, views.at[v], view_sem.at[v])
+        for v, ref in enumerate((one_hbm, two_hbm))
+    ]
+    for copy in fetch:
+        copy.start()
     load = pltpu.make_async_copy(weight_hbm, weight, weight_sem)
     load.start()
 
@@ -64,8 +71,9 @@
     def _():
         pl.semaphore_signal(barrier, inc=1, device_id=outer, device_id_type=MESH)
 
-    for v, ref in enumerate((one_ref, two_ref)):
-        x = ref[...].astype(f32)
+    for v in range(2):
+        fetch[v].wait()
+        x = views[v].astype(f32)
         mean = jnp.sum(x, axis=0, keepdims=True) / rows
         x = x - mean
         stat[0, pl.ds(2 * v, 1)] = mean
@@ -80,14 +88,14 @@
         stat_copy(r).start()
     for r in range(1, DP):
         stat_copy(r).wait_recv()
-    for v, ref in enumerate((one_ref, two_ref)):
+    for v in range(2):
         means = [stat[r, pl.ds(2 * v, 1)] for r in range(DP)]
         mean = sum(means) / DP
         square = sum(stat[r, pl.ds(2 * v + 1, 1)] for r in range(DP))
         square = square + rows * sum((one - mean) * (one - mean) for one in means)
         inverse = lax.rsqrt(square / total_rows + EPSILON)
         inverse_ref[pl.ds(v, 1)] = inverse
-        norm[v, pl.ds(0, rows)] = ((ref[...].astype(f32) - mean) * inverse).astype(bf16)
+        norm[v, pl.ds(0, rows)] = ((views[v].astype(f32) - mean) * inverse).astype(bf16)
 
     def norm_copy(v, src, dst, via):
         return remote(
@@ -273,6 +281,11 @@
 
         @pl.when(jnp.logical_and(is_end, j > 0))
         def _():
+            @pl.when(step >= AHEAD)
+            def _():
+                before = step - AHEAD
+                outward(MP - 1 - lax.div(before, PARTS), lax.rem(before, PARTS)).wait_send()
+
             outward(j, c).start()
 
     def finish(c, value):
@@ -328,9 +341,8 @@
 
     @pl.when(is_end)
     def _():
-        for c in range(PARTS):
-            for j in (1, 2, 3):
-                outward(j, c).wait_send()
+        for step in range((MP - 1) * PARTS - AHEAD, (MP - 1) * PARTS):
+            outward(MP - 1 - step // PARTS, step % PARTS).wait_send()
 
 
 def local_fused(view_one, view_two, proj_weight):
@@ -343,9 +355,10 @@
     return pl.pallas_call(
         fused,
         out_shape=(out, out),
-        in_specs=[vmem, vmem, pl.BlockSpec(memory_space=pl.ANY)],
+        in_specs=[pl.BlockSpec(memory_space=pl.ANY)] * 3,
         out_specs=(vmem, vmem),
         scratch_shapes=[
+            pltpu.VMEM((2, rows, width), bf16),
             pltpu.VMEM(proj_weight.shape, bf16),
             pltpu.VMEM((2, DP * rows, width), bf16),
             pltpu.VMEM((DP, 4, width), f32),
@@ -361,6 +374,7 @@
             pltpu.VMEM((MP, PARTS, 2 * rows, slim), bf16),
             pltpu.VMEM((MP, PARTS, 2 * rows, slim), bf16),
             pltpu.VMEM((2, PARTS, 2 * rows, slim), bf16),
+            dma((2,)),
             dma(()),
             dma((DP,)), dma((DP,)), dma((DP,)), dma((DP,)),
             dma((DP, 2)), dma((DP, 2)),

time: 88.2 us -> 88.3 us (level)
  no operation moved by 1% of the time
where the time goes in v3:
time: 88.3 us; the launch traced here: 88.2 us
  Pallas kernels  84.2 us (95%)
  local copies, waits for them, and re-layouts  3.3 us (4%)
    pallas_call x1, Pallas kernels, local_fused(): pl.pallas_call(fused, out_shape=(out, out), in_specs=[pl.BlockSpec(memory...  84.2 us
    unnamed x6, local copies, waits for them, and re-layouts  3.3 us

profile of v3, /device:TPU:0, one launch (start us, length us, event | category | flops | bytes accessed | tf_op | source)
XLA Modules:
  0.0 88.2 jit_solution(3116190670956740139)
XLA Ops:
  0.6 0.0 copy-start
  0.6 0.9 %copy-done = bf16[128,1024]{1,0:T(8,128)(2,1)S(1)} copy-done((bf16[128,1024]{1,0:T(8,128)(2,1)S(1)}, bf16[128,1024]{1,0:T(8,128)(2,1)}, u32[]{:S(2)}) %copy-start) | copy-done | bytes 262168
  1.6 0.0 copy-start.1
  1.6 0.9 %copy-done.1 = bf16[128,1024]{1,0:T(8,128)(2,1)S(1)} copy-done((bf16[128,1024]{1,0:T(8,128)(2,1)S(1)}, bf16[128,1024]{1,0:T(8,128)(2,1)}, u32[]{:S(2)}) %copy-start.1) | copy-done | bytes 262168
  2.5 84.2 %shard_map.50 = (bf16[128,1024]{1,0:T(8,128)(2,1)S(1)}, bf16[128,1024]{1,0:T(8,128)(2,1)S(1)}) custom-call(bf16[128,1024]{1,0:T(8,128)(2,1)S(1)} %copy-done, bf16[128,1024]{1,0:T(8,128)(2,1)S(1)} %copy-done.1, bf16[4096,1024]{1,0:T(8,128)(2,1)} %weight_hbm.1), custom_call_target="tpu_custom_call" | custom-call | flops 3221225472 | bytes 9437184 | tf_op jit(solution)/shard_map/pallas_call | solution.py:355
  86.8 0.7 copy.7
  87.5 0.7 copy.8
Async XLA Ops:
  0.6 1.0 %copy-start = (bf16[128,1024]{1,0:T(8,128)(2,1)S(1)}, bf16[128,1024]{1,0:T(8,128)(2,1)}, u32[]{:S(2)}) copy-start(bf16[128,1024]{1,0:T(8,128)(2,1)} %one_hbm.1) | copy-start | bytes 786436
  1.6 0.9 %copy-start.1 = (bf16[128,1024]{1,0:T(8,128)(2,1)S(1)}, bf16[128,1024]{1,0:T(8,128)(2,1)}, u32[]{:S(2)}) copy-start(bf16[128,1024]{1,0:T(8,128)(2,1)} %two_hbm.1) | copy-start | bytes 786436

commit v4 on v0

--- a/solution.py
+++ b/solution.py
@@ -1,10 +1,442 @@
 import jax
 import jax.numpy as jnp
 from jax import lax
+from jax.experimental import pallas as pl
+from jax.experimental.pallas import tpu as pltpu
 from jax.sharding import PartitionSpec as P
 
 OFF_WEIGHT = 0.0125
 EPSILON = 1e-05
+MESH = pl.DeviceIdType.MESH
+DP, MP = 8, 4
+VMEM_MIB = 60
+PARTS = 4
+
+
+def times_t(left, right):
+    return lax.dot_general(
+        left, right, (((1,), (1,)), ((), ())), preferred_element_type=jnp.float32
+    )
+
+
+def fused(
+    one_hbm, two_hbm, weight_hbm, grad_one_ref, grad_two_ref,
+    weight, raw, norm, stat, back, inverse_ref, mean_ref, diagonal, up, own_gram, from_end, from_mid,
+    gram, delta, part, from_outer, from_inner,
+    view_sem, weight_sem, stat_s, stat_r, back_s, back_r, raw_s, raw_r,
+    gram_s, end_r, mid_r, total_s, total_r, part_s, outer_r, inner_r,
+):
+    rows, width = one_hbm.shape
+    total_rows = rows * DP
+    half = rows // 2
+    bf16, f32 = jnp.bfloat16, jnp.float32
+    a, m = lax.axis_index("dp"), lax.axis_index("mp")
+    core, along_x, along_y = lax.rem(a, 2), lax.rem(lax.div(a, 2), 2), lax.div(a, 4)
+
+    def peer(r):
+        at = a
+        if r & 1:
+            at = at + 1 - 2 * core
+        if r & 2:
+            at = at + 2 - 4 * along_x
+        if r & 4:
+            at = at + 4 - 8 * along_y
+        return (at, m)
+
+    low = m < 2
+    is_mid = jnp.logical_and(m > 0, m < MP - 1)
+    is_end = jnp.logical_not(is_mid)
+    inner = (a, jnp.where(low, m + 1, m - 1))
+    outer = (a, jnp.where(low, jnp.maximum(m - 1, 0), jnp.minimum(m + 1, MP - 1)))
+
+    def remote(src, dst, send, recv, to):
+        return pltpu.make_async_remote_copy(
+            src_ref=src, dst_ref=dst, send_sem=send, recv_sem=recv, device_id=to, device_id_type=MESH
+        )
+
+    fetch = [
+        pltpu.make_async_copy(ref, raw.at[v, pl.ds(0, rows)], view_sem.at[v])
+        for v, ref in enumerate((one_hbm, two_hbm))
+    ]
+    fetch[1].start()
+    fetch[0].start()
+    load = pltpu.make_async_copy(weight_hbm, weight, weight_sem)
+    load.start()
+
+    barrier = pltpu.get_barrier_semaphore()
+    for r in range(1, DP):
+        pl.semaphore_signal(barrier, inc=1, device_id=peer(r), device_id_type=MESH)
+    pl.semaphore_signal(barrier, inc=1, device_id=inner, device_id_type=MESH)
+
+    @pl.when(is_mid)
+    def _():
+        pl.semaphore_signal(barrier, inc=1, device_id=outer, device_id_type=MESH)
+
+    def raw_copy(v, src, dst, via, h=None):
+        size = rows if h is None else half
+        skip = 0 if h is None else h * half
+        return remote(
+            raw.at[v, pl.ds(src * rows + skip, size)], raw.at[v, pl.ds(dst * rows + skip, size)],
+            raw_s.at[dst, v, h or 0], raw_r.at[dst, v, h or 0], peer(via),
+        )
+
+    def got(v, slot, h=None):
+        raw_copy(v, slot, slot, 1, h).wait_recv()
+
+    sent = []
+
+    def give(v, src, dst, via, h=None):
+        copy = raw_copy(v, src, dst, via, h)
+        copy.start()
+        sent.append(copy)
+
+    def give_own(v):
+        give(v, 0, 2, 2, 0)
+        give(v, 0, 4, 4, 1)
+        give(v, 0, 1, 1)
+        give(v, 0, 2, 2, 1)
+        give(v, 0, 4, 4, 0)
+
+    def give_across(v):
+        got(v, 2, 0)
+        give(v, 2, 6, 4, 0)
+        got(v, 4, 1)
+        give(v, 4, 6, 2, 1)
+
+    def block_stat(v):
+        x = raw[v, pl.ds(0, rows)].astype(f32)
+        mean = jnp.sum(x, axis=0, keepdims=True) / rows
+        x = x - mean
+        stat[0, pl.ds(2 * v, 1)] = mean
+        stat[0, pl.ds(2 * v + 1, 1)] = jnp.sum(x * x, axis=0, keepdims=True)
+
+    def stat_copy(r):
+        return remote(stat.at[0], stat.at[r], stat_s.at[r], stat_r.at[r], peer(r))
+
+    for v in (1, 0):
+        fetch[v].wait()
+        block_stat(v)
+    pl.semaphore_wait(barrier, DP + jnp.where(is_mid, 1, 0))
+    for r in range(DP - 1, 0, -1):
+        stat_copy(r).start()
+    give_own(1)
+    for r in range(1, DP):
+        stat_copy(r).wait_recv()
+    for v in range(2):
+        means = [stat[r, pl.ds(2 * v, 1)] for r in range(DP)]
+        mean = sum(means) / DP
+        square = sum(stat[r, pl.ds(2 * v + 1, 1)] for r in range(DP))
+        square = square + rows * sum((one - mean) * (one - mean) for one in means)
+        mean_ref[pl.ds(v, 1)] = mean
+        inverse_ref[pl.ds(v, 1)] = lax.rsqrt(square / total_rows + EPSILON)
+
+    def normalize(v, slot):
+        x = raw[v, pl.ds(slot * rows, rows)].astype(f32)
+        norm[v, pl.ds(slot * rows, rows)] = (
+            (x - mean_ref[pl.ds(v, 1)]) * inverse_ref[pl.ds(v, 1)]
+        ).astype(bf16)
+
+    chunks = ((1, 0), (1, 1), (1, 2), (1, 3), (0, 0), (0, 1), (0, 2), (0, 3))
+    wide = 2 * rows
+
+    def end_copy(k):
+        return remote(own_gram.at[k], from_end.at[k], gram_s.at[k], end_r.at[k], inner)
+
+    def mid_copy(k):
+        return remote(own_gram.at[k], from_mid.at[k], gram_s.at[k], mid_r.at[k], inner)
+
+    def total_copy(k):
+        return remote(gram.at[k], gram.at[k], total_s.at[k], total_r.at[k], outer)
+
+    def own(k):
+        v, p = chunks[k]
+        own_gram[k] = times_t(norm[v, pl.ds(0, rows)], norm[v, pl.ds(p * wide, wide)]).astype(bf16)
+
+        @pl.when(is_end)
+        def _():
+            end_copy(k).start()
+
+    def across(k):
+        @pl.when(is_mid)
+        def _():
+            end_copy(k).wait_recv()
+            own_gram[k] = (own_gram[k].astype(f32) + from_end[k].astype(f32)).astype(bf16)
+            mid_copy(k).start()
+
+    def back_out(k):
+        @pl.when(is_mid)
+        def _():
+            mid_copy(k).wait_recv()
+            gram[k] = (own_gram[k].astype(f32) + from_mid[k].astype(f32)).astype(bf16)
+            total_copy(k).start()
+
+    def use(k):
+        v, p = chunks[k]
+
+        @pl.when(is_end)
+        def _():
+            total_copy(k).wait_recv()
+
+        product = jnp.dot(gram[k], norm[1 - v, pl.ds(p * wide, wide)], preferred_element_type=f32)
+        if p == 0:
+            up[1 - v] = product
+        else:
+            up[1 - v] += product
+
+    def match(p):
+        both = norm[0, pl.ds(p * wide, wide)].astype(f32) * norm[1, pl.ds(p * wide, wide)].astype(f32)
+        both = jnp.sum(both, axis=0, keepdims=True)
+        diagonal[pl.ds(0, 1)] = both if p == 0 else diagonal[pl.ds(0, 1)] + both
+
+    def back_copy(v, r):
+        return remote(back.at[v, 0], back.at[v, r], back_s.at[v, r], back_r.at[v, r], peer(r))
+
+    def upstream(v):
+        diag = diagonal[pl.ds(0, 1)] / total_rows
+        slope = 2.0 * (diag - 1.0) - 2.0 * OFF_WEIGHT * diag
+        mine = norm[v, pl.ds(0, rows)].astype(f32)
+        other = norm[1 - v, pl.ds(0, rows)].astype(f32)
+        value = up[v] * (2.0 * OFF_WEIGHT / total_rows) + other * slope
+        up[v] = value
+        back[v, 0, pl.ds(0, 1)] = jnp.sum(value, axis=0, keepdims=True)
+        back[v, 0, pl.ds(1, 1)] = jnp.sum(value * mine, axis=0, keepdims=True)
+        for r in range(DP - 1, 0, -1):
+            back_copy(v, r).start()
+
+    def through_norm(v):
+        for r in range(1, DP):
+            back_copy(v, r).wait_recv()
+        mean_up = sum(back[v, r, pl.ds(0, 1)] for r in range(DP)) / total_rows
+        cross = sum(back[v, r, pl.ds(1, 1)] for r in range(DP)) / total_rows
+        mine = norm[v, pl.ds(0, rows)].astype(f32)
+        delta[v] = (inverse_ref[pl.ds(v, 1)] * (up[v] - mean_up - mine * cross)).astype(bf16)
+
+    slim = width // PARTS
+
+    def outward(v, j, c):
+        return remote(
+            part.at[v, j, c], from_outer.at[v, j, c], part_s.at[v, j, c], outer_r.at[v, j, c], inner
+        )
+
+    def over(v, j, c):
+        return remote(
+            part.at[v, j, c], from_inner.at[v, 3 - j, c], part_s.at[v, j, c], inner_r.at[v, 3 - j, c], inner
+        )
+
+    def homeward(v, c):
+        return remote(
+            part.at[v, 0, c], from_inner.at[v, 0, c], part_s.at[v, 0, c], inner_r.at[v, 0, c], outer
+        )
+
+    def products(v):
+        @pl.loop(0, MP * PARTS)
+        def _(step):
+            j = MP - 1 - lax.div(step, PARTS)
+            c = lax.rem(step, PARTS)
+            block = jnp.where(low, j, MP - 1 - j)
+            start = pl.multiple_of(block * width + c * slim, slim)
+            part[v, j, c] = times_t(delta[v], weight[pl.ds(start, slim)]).astype(bf16)
+
+            @pl.when(jnp.logical_and(is_end, j > 0))
+            def _():
+                outward(v, j, c).start()
+
+    normalize(1, 0)
+    got(1, 1)
+    normalize(1, 1)
+    own(0)
+    give_across(1)
+    give_own(0)
+    got(1, 2, 1)
+    give(1, 2, 3, 1)
+    got(1, 4, 0)
+    give(1, 4, 5, 1)
+    normalize(1, 2)
+    normalize(1, 4)
+    across(0)
+    got(1, 3)
+    normalize(1, 3)
+    own(1)
+    got(1, 5)
+    normalize(1, 5)
+    own(2)
+    back_out(0)
+    normalize(0, 0)
+    got(0, 1)
+    normalize(0, 1)
+    got(1, 6, 0)
+    got(1, 6, 1)
+    give(1, 6, 7, 1)
+    normalize(1, 6)
+    across(1)
+    across(2)
+    got(1, 7)
+    normalize(1, 7)
+    own(3)
+    own(4)
+    back_out(1)
+    back_out(2)
+    match(0)
+
+    give_across(0)
+    use(0)
+    across(3)
+    across(4)
+    got(0, 2, 1)
+    give(0, 2, 3, 1)
+    got(0, 4, 0)
+    give(0, 4, 5, 1)
+    normalize(0, 2)
+    normalize(0, 4)
+    back_out(3)
+    back_out(4)
+    got(0, 3)
+    normalize(0, 3)
+    own(5)
+    use(1)
+    got(0, 5)
+    normalize(0, 5)
+    own(6)
+    use(2)
+    match(1)
+    match(2)
+    across(5)
+    across(6)
+    got(0, 6, 0)
+    got(0, 6, 1)
+    give(0, 6, 7, 1)
+    normalize(0, 6)
+    got(0, 7)
+    normalize(0, 7)
+    match(3)
+    use(3)
+    upstream(0)
+    own(7)
+    back_out(5)
+    back_out(6)
+    load.wait()
+    through_norm(0)
+    products(0)
+
+    across(7)
+    use(4)
+    use(5)
+    use(6)
+    back_out(7)
+    use(7)
+    upstream(1)
+    through_norm(1)
+    products(1)
+
+    outs = (grad_one_ref, grad_two_ref)
+
+    @pl.when(is_end)
+    def _():
+        for v in range(2):
+            for c in range(PARTS):
+                homeward(v, c).wait_recv()
+                outs[v][:, pl.ds(c * slim, slim)] = (
+                    part[v, 0, c].astype(f32) + from_inner[v, 0, c].astype(f32)
+                ).astype(bf16)
+
+    @pl.when(is_mid)
+    def _():
+        def pass_on(v, j, c):
+            outward(v, j, c).wait_recv()
+            part[v, j, c] = (part[v, j, c].astype(f32) + from_outer[v, j, c].astype(f32)).astype(bf16)
+            over(v, j, c).start()
+
+        def pass_home(v, c):
+            over(v, 3, c).wait_recv()
+            part[v, 0, c] = (part[v, 0, c].astype(f32) + from_inner[v, 0, c].astype(f32)).astype(bf16)
+            homeward(v, c).start()
+
+        for v in range(2):
+            order = [(3, c) for c in range(PARTS)] + [(2, c) for c in range(PARTS)]
+            for at, (j, c) in enumerate(order):
+                pass_on(v, j, c)
+                if 2 <= at < PARTS + 2:
+                    pass_home(v, at - 2)
+            for c in range(PARTS):
+                over(v, 2, c).wait_recv()
+                outward(v, 1, c).wait_recv()
+                outs[v][:, pl.ds(c * slim, slim)] = (
+                    part[v, 1, c].astype(f32) + from_outer[v, 1, c].astype(f32)
+                    + from_inner[v, 1, c].astype(f32)
+                ).astype(bf16)
+
+    for r in range(1, DP):
+        stat_copy(r).wait_send()
+        for v in range(2):
+            back_copy(v, r).wait_send()
+    for copy in sent:
+        copy.wait_send()
+    for k in range(len(chunks)):
+        end_copy(k).wait_send()
+
+    @pl.when(is_mid)
+    def _():
+        for k in range(len(chunks)):
+            total_copy(k).wait_send()
+        for v in range(2):
+            for c in range(PARTS):
+                for j in (0, 2, 3):
+                    outward(v, j, c).wait_send()
+
+    @pl.when(is_end)
+    def _():
+        for v in range(2):
+            for c in range(PARTS):
+                for j in (1, 2, 3):
+                    outward(v, j, c).wait_send()
+
+
+def local_fused(view_one, view_two, proj_weight):
+    rows, width = view_one.shape
+    bf16, f32 = jnp.bfloat16, jnp.float32
+    dma = pltpu.SemaphoreType.DMA
+    slim = width // PARTS
+    out = jax.ShapeDtypeStruct((rows, width), bf16)
+    vmem = pl.BlockSpec(memory_space=pltpu.VMEM)
+    return pl.pallas_call(
+        fused,
+        out_shape=(out, out),
+        in_specs=[pl.BlockSpec(memory_space=pl.ANY)] * 3,
+        out_specs=(vmem, vmem),
+        scratch_shapes=[
+            pltpu.VMEM(proj_weight.shape, bf16),
+            pltpu.VMEM((2, DP * rows, width), bf16),
+            pltpu.VMEM((2, DP * rows, width), bf16),
+            pltpu.VMEM((DP, 4, width), f32),
+            pltpu.VMEM((2, DP, 2, width), f32),
+            pltpu.VMEM((8, width), f32),
+            pltpu.VMEM((8, width), f32),
+            pltpu.VMEM((8, width), f32),
+            pltpu.VMEM((2, rows, width), f32),
+            pltpu.VMEM((8, rows, 2 * rows), bf16),
+            pltpu.VMEM((8, rows, 2 * rows), bf16),
+            pltpu.VMEM((8, rows, 2 * rows), bf16),
+            pltpu.VMEM((8, rows, 2 * rows), bf16),
+            pltpu.VMEM((2, rows, width), bf16),
+            pltpu.VMEM((2, MP, PARTS, rows, slim), bf16),
+            pltpu.VMEM((2, MP, PARTS, rows, slim), bf16),
+            pltpu.VMEM((2, 2, PARTS, rows, slim), bf16),
+            dma((2,)),
+            dma(()),
+            dma((DP,)), dma((DP,)), dma((2, DP)), dma((2, DP)),
+            dma((DP, 2, 2)), dma((DP, 2, 2)),
+            dma((8,)), dma((8,)), dma((8,)), dma((8,)), dma((8,)),
+            dma((2, MP, PARTS)), dma((2, MP, PARTS)), dma((2, 2, PARTS)),
+        ],
+        compiler_params=pltpu.CompilerParams(
+            collective_id=0, has_side_effects=True, vmem_limit_bytes=VMEM_MIB * 1024 * 1024
+        ),
+        cost_estimate=pl.CostEstimate(
+            flops=4 * rows * width * (2 * DP * rows + MP * width),
+            bytes_accessed=2 * (MP * width * width + 4 * rows * width),
+            transcendentals=0,
+        ),
+    )(view_one, view_two, proj_weight)
 
 
 def contract_rows(left, right):
@@ -97,6 +529,14 @@
 
 def solution(mesh):
     placed = (P("dp", "mp"), P("dp", "mp"), P(None, "mp"))
-    return jax.shard_map(
-        local, mesh=mesh, in_specs=placed, out_specs=(P("dp", "mp"), P("dp", "mp")), check_vma=False
-    )
+
+    def whole(view_one, view_two, proj_weight):
+        batch, features = view_one.shape
+        suits = dict(mesh.shape) == {"dp": DP, "mp": MP}
+        suits = suits and batch % (DP * 128) == 0 and 2 * batch <= features and features <= 4096
+        return jax.shard_map(
+            local_fused if suits else local,
+            mesh=mesh, in_specs=placed, out_specs=(P("dp", "mp"), P("dp", "mp")), check_vma=False,
+        )(view_one, view_two, proj_weight)
+
+    return whole

time: 378 us -> 83.7 us (0.22)
  waiting for transfers between devices: 265 us -> 0 us
  Pallas kernels: 0 us -> 79.6 us
  blocking collectives: 51.4 us -> 0 us
  matrix products: 36.2 us -> 0 us
  between operations: 14.2 us -> 0.64 us
  other arithmetic: 10.1 us -> 0 us
    reduce_scatter x4 -> x0, waiting for transfers between devices: 182 us -> none  [the longest x1 116 us: local(): lax.psum_scatter(corr_part, 'dp', scatter_dimension=1, tiled=True)]
    all_gather x2 -> x0, waiting for transfers between devices: 83.4 us -> none  [the longest x1 56 us: local(): piece = lax.all_gather(grad_shard, 'dp', axis=1, tiled=True)]
    pallas_call x0 -> x1, Pallas kernels: none -> 79.6 us  [local_fused(): pl.pallas_call(fused, out_shape=(out, out), in_specs=[pl.BlockSpec(memory...]
    psum x3 -> x0, blocking collectives: 51.4 us -> none  [the longest x1 23.8 us: local(): lax.psum((jnp.sum(upper, axis=0), jnp.sum(upper * normal_one, axis=0), jn...]
    dot_general x5 -> x0, matrix products: 36.2 us -> none  [the longest x3 21.1 us: times_transposed(): lax.dot_general(left, right, (((1,), (1,)), ((), ())), preferred_element_...]
    reduce_sum x5 -> x0, other arithmetic: 5.17 us -> none  [the longest x1 1.09 us: local(): jnp.sum(up_two, axis=0)]
    convert_element_type x2 -> x0, other arithmetic: 4.86 us -> none  [the longest x1 3.13 us: local(): grad_shard = jnp.where(row_ids == col_ids, -2.0 * (1.0 - corr_shard), 2.0...]
  transfers between devices with their start and end apart: 6 -> 0, of which waited for: 6 -> 0; matrix products, arithmetic and copies ran while one was open for 4% -> 0% of each run, Pallas kernels for 0% -> 0%
where the time goes in v4:
time: 83.7 us; the launch traced here: 83.6 us
  Pallas kernels  79.6 us (95%)
  local copies, waits for them, and re-layouts  3.34 us (4%)
    pallas_call x1, Pallas kernels, local_fused(): pl.pallas_call(fused, out_shape=(out, out), in_specs=[pl.BlockSpec(memory...  79.6 us
    unnamed x2, local copies, waits for them, and re-layouts  3.34 us

profile of v4, /device:TPU:0, one launch (start us, length us, event | category | flops | bytes accessed | tf_op | source)
XLA Modules:
  0.0 83.6 jit_solution(4271745738708385687)
XLA Ops:
  0.6 79.6 %shard_map.50 = (bf16[128,1024]{1,0:T(8,128)(2,1)}, bf16[128,1024]{1,0:T(8,128)(2,1)}) custom-call(bf16[128,1024]{1,0:T(8,128)(2,1)} %one_hbm.1, bf16[128,1024]{1,0:T(8,128)(2,1)} %two_hbm.1, bf16[4096,1024]{1,0:T(8,128)(2,1)} %weight_hbm.1), custom_call_target="tpu_custom_call" | custom-call | flops 3221225472 | bytes 9437184 | tf_op jit(solution)/shard_map/pallas_call | solution.py:401
  80.2 1.7 %copy.7 = bf16[128,1024]{1,0:T(8,128)(2,1)} copy(bf16[128,1024]{1,0:T(8,128)(2,1)} %get-tuple-element.4) | data formatting | bytes 524288
  81.9 1.7 %copy.8 = bf16[128,1024]{1,0:T(8,128)(2,1)} copy(bf16[128,1024]{1,0:T(8,128)(2,1)} %get-tuple-element.5) | data formatting | bytes 524288

commit v5 on v4

--- a/solution.py
+++ b/solution.py
@@ -9,7 +9,7 @@
 EPSILON = 1e-05
 MESH = pl.DeviceIdType.MESH
 DP, MP = 8, 4
-VMEM_MIB = 60
+VMEM_MIB = 48
 PARTS = 4
 
 
@@ -240,6 +240,16 @@
             @pl.when(jnp.logical_and(is_end, j > 0))
             def _():
                 outward(v, j, c).start()
+
+    def pass_on(v, j, c):
+        outward(v, j, c).wait_recv()
+        part[v, j, c] = (part[v, j, c].astype(f32) + from_outer[v, j, c].astype(f32)).astype(bf16)
+        over(v, j, c).start()
+
+    def pass_home(v, c):
+        over(v, 3, c).wait_recv()
+        part[v, 0, c] = (part[v, 0, c].astype(f32) + from_inner[v, 0, c].astype(f32)).astype(bf16)
+        homeward(v, c).start()
 
     normalize(1, 0)
     got(1, 1)
@@ -325,6 +335,12 @@
     back_out(7)
     use(7)
     upstream(1)
+
+    @pl.when(is_mid)
+    def _():
+        for c in range(PARTS):
+            pass_on(0, MP - 1, c)
+
     through_norm(1)
     products(1)
 
@@ -341,22 +357,13 @@
 
     @pl.when(is_mid)
     def _():
-        def pass_on(v, j, c):
-            outward(v, j, c).wait_recv()
-            part[v, j, c] = (part[v, j, c].astype(f32) + from_outer[v, j, c].astype(f32)).astype(bf16)
-            over(v, j, c).start()
-
-        def pass_home(v, c):
-            over(v, 3, c).wait_recv()
-            part[v, 0, c] = (part[v, 0, c].astype(f32) + from_inner[v, 0, c].astype(f32)).astype(bf16)
-            homeward(v, c).start()
-
         for v in range(2):
-            order = [(3, c) for c in range(PARTS)] + [(2, c) for c in range(PARTS)]
-            for at, (j, c) in enumerate(order):
-                pass_on(v, j, c)
-                if 2 <= at < PARTS + 2:
-                    pass_home(v, at - 2)
+            if v == 1:
+                for c in range(PARTS):
+                    pass_on(v, MP - 1, c)
+            for c in range(PARTS):
+                pass_home(v, c)
+                pass_on(v, MP - 2, c)
             for c in range(PARTS):
                 over(v, 2, c).wait_recv()
                 outward(v, 1, c).wait_recv()
@@ -401,7 +408,7 @@
     return pl.pallas_call(
         fused,
         out_shape=(out, out),
-        in_specs=[pl.BlockSpec(memory_space=pl.ANY)] * 3,
+        in_specs=[pl.BlockSpec(memory_space=pltpu.HBM)] * 3,
         out_specs=(vmem, vmem),
         scratch_shapes=[
             pltpu.VMEM(proj_weight.shape, bf16),

time: 83.7 us -> 77.3 us (0.924)
  Pallas kernels: 79.6 us -> 73.2 us
    pallas_call x1, Pallas kernels: 79.6 us -> 73.2 us  [local_fused(): pl.pallas_call(fused, out_shape=(out, out), in_specs=[pl.BlockSpec(memory...]
    unnamed x2 -> x6, local copies, waits for them, and re-layouts: 3.34 us -> 3.3 us
where the time goes in v5:
time: 77.3 us; the launch traced here: 77.2 us
  Pallas kernels  73.2 us (95%)
  local copies, waits for them, and re-layouts  3.3 us (4%)
    pallas_call x1, Pallas kernels, local_fused(): pl.pallas_call(fused, out_shape=(out, out), in_specs=[pl.BlockSpec(memory...  73.2 us
    unnamed x6, local copies, waits for them, and re-layouts  3.3 us

profile of v5, /device:TPU:0, one launch (start us, length us, event | category | flops | bytes accessed | tf_op | source)
XLA Modules:
  0.0 77.2 jit_solution(5779029616392829346)
XLA Ops:
  0.6 0.0 copy-start
  0.6 0.9 %copy-done = bf16[128,1024]{1,0:T(8,128)(2,1)S(1)} copy-done((bf16[128,1024]{1,0:T(8,128)(2,1)S(1)}, bf16[128,1024]{1,0:T(8,128)(2,1)}, u32[]{:S(2)}) %copy-start) | copy-done | bytes 262168
  1.6 0.0 copy-start.1
  1.6 0.9 %copy-done.1 = bf16[128,1024]{1,0:T(8,128)(2,1)S(1)} copy-done((bf16[128,1024]{1,0:T(8,128)(2,1)S(1)}, bf16[128,1024]{1,0:T(8,128)(2,1)}, u32[]{:S(2)}) %copy-start.1) | copy-done | bytes 262168
  2.5 73.2 %shard_map.50 = (bf16[128,1024]{1,0:T(8,128)(2,1)S(1)}, bf16[128,1024]{1,0:T(8,128)(2,1)S(1)}) custom-call(bf16[128,1024]{1,0:T(8,128)(2,1)S(1)} %copy-done, bf16[128,1024]{1,0:T(8,128)(2,1)S(1)} %copy-done.1, bf16[4096,1024]{1,0:T(8,128)(2,1)} %weight_hbm.1), custom_call_target="tpu_custom_call" | custom-call | flops 3221225472 | bytes 9437184 | tf_op jit(solution)/shard_map/pallas_call | solution.py:408
  75.7 0.7 copy.7
  76.5 0.7 copy.8
Async XLA Ops:
  0.6 1.0 %copy-start = (bf16[128,1024]{1,0:T(8,128)(2,1)S(1)}, bf16[128,1024]{1,0:T(8,128)(2,1)}, u32[]{:S(2)}) copy-start(bf16[128,1024]{1,0:T(8,128)(2,1)} %one_hbm.1) | copy-start | bytes 786436
  1.6 0.9 %copy-start.1 = (bf16[128,1024]{1,0:T(8,128)(2,1)S(1)}, bf16[128,1024]{1,0:T(8,128)(2,1)}, u32[]{:S(2)}) copy-start(bf16[128,1024]{1,0:T(8,128)(2,1)} %two_hbm.1) | copy-start | bytes 786436

commit v6 on v5

--- a/solution.py
+++ b/solution.py
@@ -9,7 +9,7 @@
 EPSILON = 1e-05
 MESH = pl.DeviceIdType.MESH
 DP, MP = 8, 4
-VMEM_MIB = 48
+VMEM_KIB = 54700
 PARTS = 4
 
 
@@ -313,10 +313,12 @@
     across(5)
     across(6)
     got(0, 6, 0)
+    give(0, 6, 7, 1, 0)
     got(0, 6, 1)
-    give(0, 6, 7, 1)
+    give(0, 6, 7, 1, 1)
     normalize(0, 6)
-    got(0, 7)
+    got(0, 7, 0)
+    got(0, 7, 1)
     normalize(0, 7)
     match(3)
     use(3)
@@ -324,15 +326,15 @@
     own(7)
     back_out(5)
     back_out(6)
+    use(4)
     load.wait()
     through_norm(0)
+    across(7)
     products(0)
 
-    across(7)
-    use(4)
+    back_out(7)
     use(5)
     use(6)
-    back_out(7)
     use(7)
     upstream(1)
 
@@ -436,7 +438,7 @@
             dma((2, MP, PARTS)), dma((2, MP, PARTS)), dma((2, 2, PARTS)),
         ],
         compiler_params=pltpu.CompilerParams(
-            collective_id=0, has_side_effects=True, vmem_limit_bytes=VMEM_MIB * 1024 * 1024
+            collective_id=0, has_side_effects=True, vmem_limit_bytes=VMEM_KIB * 1024
         ),
         cost_estimate=pl.CostEstimate(
             flops=4 * rows * width * (2 * DP * rows + MP * width),

time: 77.3 us -> 73.5 us (0.951)
  Pallas kernels: 73.2 us -> 71.1 us
  local copies, waits for them, and re-layouts: 3.3 us -> 1.41 us
    pallas_call x1, Pallas kernels: 73.2 us -> 71.1 us  [local_fused(): pl.pallas_call(fused, out_shape=(out, out), in_specs=[pl.BlockSpec(memory...]
    unnamed x6 -> x2, local copies, waits for them, and re-layouts: 3.3 us -> 1.41 us
where the time goes in v6:
time: 73.5 us; the launch traced here: 73.1 us
  Pallas kernels  71.1 us (97%)
  local copies, waits for them, and re-layouts  1.41 us (2%)
    pallas_call x1, Pallas kernels, local_fused(): pl.pallas_call(fused, out_shape=(out, out), in_specs=[pl.BlockSpec(memory...  71.1 us

profile of v6, /device:TPU:0, one launch (start us, length us, event | category | flops | bytes accessed | tf_op | source)
XLA Modules:
  0.0 73.1 jit_solution(29781976652947627)
XLA Ops:
  0.6 71.1 %shard_map.50 = (bf16[128,1024]{1,0:T(8,128)(2,1)S(1)}, bf16[128,1024]{1,0:T(8,128)(2,1)S(1)}) custom-call(bf16[128,1024]{1,0:T(8,128)(2,1)} %one_hbm.1, bf16[128,1024]{1,0:T(8,128)(2,1)} %two_hbm.1, bf16[4096,1024]{1,0:T(8,128)(2,1)} %weight_hbm.1), custom_call_target="tpu_custom_call" | custom-call | flops 3221225472 | bytes 9437184 | tf_op jit(solution)/shard_map/pallas_call | solution.py:410
  71.7 0.7 copy.7
  72.4 0.7 copy.8

commit v7 on v6

--- a/solution.py
+++ b/solution.py
@@ -170,21 +170,27 @@
             gram[k] = (own_gram[k].astype(f32) + from_mid[k].astype(f32)).astype(bf16)
             total_copy(k).start()
 
-    def use(k):
+    def use(k, slots=(0, 1)):
         v, p = chunks[k]
 
-        @pl.when(is_end)
-        def _():
-            total_copy(k).wait_recv()
-
-        product = jnp.dot(gram[k], norm[1 - v, pl.ds(p * wide, wide)], preferred_element_type=f32)
+        if slots[0] == 0:
+            @pl.when(is_end)
+            def _():
+                total_copy(k).wait_recv()
+
+        skip, size = slots[0] * rows, len(slots) * rows
+        product = jnp.dot(
+            gram[k, :, pl.ds(skip, size)], norm[1 - v, pl.ds(p * wide + skip, size)],
+            preferred_element_type=f32,
+        )
         if p == 0:
             up[1 - v] = product
         else:
             up[1 - v] += product
 
-    def match(p):
-        both = norm[0, pl.ds(p * wide, wide)].astype(f32) * norm[1, pl.ds(p * wide, wide)].astype(f32)
+    def match(p, slots=(0, 1)):
+        at = pl.ds(p * wide + slots[0] * rows, len(slots) * rows)
+        both = norm[0, at].astype(f32) * norm[1, at].astype(f32)
         both = jnp.sum(both, axis=0, keepdims=True)
         diagonal[pl.ds(0, 1)] = both if p == 0 else diagonal[pl.ds(0, 1)] + both
 
@@ -284,11 +290,11 @@
     normalize(1, 7)
     own(3)
     own(4)
+    match(0)
+
+    give_across(0)
     back_out(1)
     back_out(2)
-    match(0)
-
-    give_across(0)
     use(0)
     across(3)
     across(4)
@@ -298,15 +304,15 @@
     give(0, 4, 5, 1)
     normalize(0, 2)
     normalize(0, 4)
-    back_out(3)
-    back_out(4)
     got(0, 3)
     normalize(0, 3)
     own(5)
+    back_out(3)
     use(1)
     got(0, 5)
     normalize(0, 5)
     own(6)
+    back_out(4)
     use(2)
     match(1)
     match(2)
@@ -317,11 +323,13 @@
     got(0, 6, 1)
     give(0, 6, 7, 1, 1)
     normalize(0, 6)
+    match(3, (0,))
+    use(3, (0,))
     got(0, 7, 0)
     got(0, 7, 1)
     normalize(0, 7)
-    match(3)
-    use(3)
+    match(3, (1,))
+    use(3, (1,))
     upstream(0)
     own(7)
     back_out(5)
@@ -348,14 +356,31 @@
 
     outs = (grad_one_ref, grad_two_ref)
 
+    def all_left():
+        for r in range(1, DP):
+            stat_copy(r).wait_send()
+            for v in range(2):
+                back_copy(v, r).wait_send()
+        for copy in sent:
+            copy.wait_send()
+        for k in range(len(chunks)):
+            end_copy(k).wait_send()
+
+    def parts_left(v, blocks):
+        for j in blocks:
+            for c in range(PARTS):
+                outward(v, j, c).wait_send()
+
     @pl.when(is_end)
     def _():
+        all_left()
         for v in range(2):
             for c in range(PARTS):
                 homeward(v, c).wait_recv()
                 outs[v][:, pl.ds(c * slim, slim)] = (
                     part[v, 0, c].astype(f32) + from_inner[v, 0, c].astype(f32)
                 ).astype(bf16)
+            parts_left(v, (3, 2, 1))
 
     @pl.when(is_mid)
     def _():
@@ -366,6 +391,11 @@
             for c in range(PARTS):
                 pass_home(v, c)
                 pass_on(v, MP - 2, c)
+            if v == 0:
+                all_left()
+                for k in range(len(chunks)):
+                    total_copy(k).wait_send()
+            parts_left(v, (3, 0))
             for c in range(PARTS):
                 over(v, 2, c).wait_recv()
                 outward(v, 1, c).wait_recv()
@@ -373,31 +403,7 @@
                     part[v, 1, c].astype(f32) + from_outer[v, 1, c].astype(f32)
                     + from_inner[v, 1, c].astype(f32)
                 ).astype(bf16)
-
-    for r in range(1, DP):
-        stat_copy(r).wait_send()
-        for v in range(2):
-            back_copy(v, r).wait_send()
-    for copy in sent:
-        copy.wait_send()
-    for k in range(len(chunks)):
-        end_copy(k).wait_send()
-
-    @pl.when(is_mid)
-    def _():
-        for k in range(len(chunks)):
-            total_copy(k).wait_send()
-        for v in range(2):
-            for c in range(PARTS):
-                for j in (0, 2, 3):
-                    outward(v, j, c).wait_send()
-
-    @pl.when(is_end)
-    def _():
-        for v in range(2):
-            for c in range(PARTS):
-                for j in (1, 2, 3):
-                    outward(v, j, c).wait_send()
+            parts_left(v, (2,))
 
 
 def local_fused(view_one, view_two, proj_weight):

time: 73.5 us -> 73.5 us (level)
  no operation moved by 1% of the time
where the time goes in v7:
time: 73.5 us; the launch traced here: 73.3 us
  Pallas kernels  71.3 us (97%)
  local copies, waits for them, and re-layouts  1.41 us (2%)
    pallas_call x1, Pallas kernels, local_fused(): pl.pallas_call(fused, out_shape=(out, out), in_specs=[pl.BlockSpec(memory...  71.3 us

profile of v7, /device:TPU:0, one launch (start us, length us, event | category | flops | bytes accessed | tf_op | source)
XLA Modules:
  0.0 73.3 jit_solution(13871466718922920261)
XLA Ops:
  0.6 71.3 %shard_map.50 = (bf16[128,1024]{1,0:T(8,128)(2,1)S(1)}, bf16[128,1024]{1,0:T(8,128)(2,1)S(1)}) custom-call(bf16[128,1024]{1,0:T(8,128)(2,1)} %one_hbm.1, bf16[128,1024]{1,0:T(8,128)(2,1)} %two_hbm.1, bf16[4096,1024]{1,0:T(8,128)(2,1)} %weight_hbm.1), custom_call_target="tpu_custom_call" | custom-call | flops 3221225472 | bytes 9437184 | tf_op jit(solution)/shard_map/pallas_call | solution.py:416
  71.9 0.7 copy.7
  72.6 0.7 copy.8

commit v8 on v7

--- a/solution.py
+++ b/solution.py
@@ -234,27 +234,31 @@
             part.at[v, 0, c], from_inner.at[v, 0, c], part_s.at[v, 0, c], inner_r.at[v, 0, c], outer
         )
 
-    def products(v):
-        @pl.loop(0, MP * PARTS)
-        def _(step):
-            j = MP - 1 - lax.div(step, PARTS)
-            c = lax.rem(step, PARTS)
-            block = jnp.where(low, j, MP - 1 - j)
-            start = pl.multiple_of(block * width + c * slim, slim)
-            part[v, j, c] = times_t(delta[v], weight[pl.ds(start, slim)]).astype(bf16)
-
-            @pl.when(jnp.logical_and(is_end, j > 0))
-            def _():
+    def product(v, j, c):
+        block = jnp.where(low, j, MP - 1 - j)
+        start = pl.multiple_of(block * width + c * slim, slim)
+        return times_t(delta[v], weight[pl.ds(start, slim)])
+
+    def send_out(v):
+        @pl.when(is_end)
+        def _():
+            @pl.loop(0, (MP - 1) * PARTS)
+            def _(step):
+                j = MP - 1 - lax.div(step, PARTS)
+                c = lax.rem(step, PARTS)
+                part[v, j, c] = product(v, j, c).astype(bf16)
                 outward(v, j, c).start()
 
     def pass_on(v, j, c):
+        mine = product(v, j, c)
         outward(v, j, c).wait_recv()
-        part[v, j, c] = (part[v, j, c].astype(f32) + from_outer[v, j, c].astype(f32)).astype(bf16)
+        part[v, j, c] = (mine + from_outer[v, j, c].astype(f32)).astype(bf16)
         over(v, j, c).start()
 
     def pass_home(v, c):
+        mine = product(v, 0, c)
         over(v, 3, c).wait_recv()
-        part[v, 0, c] = (part[v, 0, c].astype(f32) + from_inner[v, 0, c].astype(f32)).astype(bf16)
+        part[v, 0, c] = (mine + from_inner[v, 0, c].astype(f32)).astype(bf16)
         homeward(v, c).start()
 
     normalize(1, 0)
@@ -338,7 +342,7 @@
     load.wait()
     through_norm(0)
     across(7)
-    products(0)
+    send_out(0)
 
     back_out(7)
     use(5)
@@ -348,11 +352,12 @@
 
     @pl.when(is_mid)
     def _():
-        for c in range(PARTS):
+        @pl.loop(0, PARTS)
+        def _(c):
             pass_on(0, MP - 1, c)
 
     through_norm(1)
-    products(1)
+    send_out(1)
 
     outs = (grad_one_ref, grad_two_ref)
 
@@ -375,34 +380,45 @@
     def _():
         all_left()
         for v in range(2):
-            for c in range(PARTS):
+            @pl.loop(0, PARTS)
+            def _(c):
+                mine = product(v, 0, c)
                 homeward(v, c).wait_recv()
-                outs[v][:, pl.ds(c * slim, slim)] = (
-                    part[v, 0, c].astype(f32) + from_inner[v, 0, c].astype(f32)
+                outs[v][:, pl.ds(pl.multiple_of(c * slim, slim), slim)] = (
+                    mine + from_inner[v, 0, c].astype(f32)
                 ).astype(bf16)
+
             parts_left(v, (3, 2, 1))
 
     @pl.when(is_mid)
     def _():
         for v in range(2):
             if v == 1:
-                for c in range(PARTS):
+                @pl.loop(0, PARTS)
+                def _(c):
                     pass_on(v, MP - 1, c)
-            for c in range(PARTS):
+
+            @pl.loop(0, PARTS)
+            def _(c):
                 pass_home(v, c)
                 pass_on(v, MP - 2, c)
+
             if v == 0:
                 all_left()
                 for k in range(len(chunks)):
                     total_copy(k).wait_send()
             parts_left(v, (3, 0))
-            for c in range(PARTS):
+
+            @pl.loop(0, PARTS)
+            def _(c):
+                mine = product(v, 1, c)
                 over(v, 2, c).wait_recv()
+                mine = mine + from_inner[v, 1, c].astype(f32)
                 outward(v, 1, c).wait_recv()
-                outs[v][:, pl.ds(c * slim, slim)] = (
-                    part[v, 1, c].astype(f32) + from_outer[v, 1, c].astype(f32)
-                    + from_inner[v, 1, c].astype(f32)
+                outs[v][:, pl.ds(pl.multiple_of(c * slim, slim), slim)] = (
+                    mine + from_outer[v, 1, c].astype(f32)
                 ).astype(bf16)
+
             parts_left(v, (2,))
 
 

time: 73.5 us -> 73.5 us (level)
  no operation moved by 1% of the time
where the time goes in v8:
time: 73.5 us; the launch traced here: 73.3 us
  Pallas kernels  71.3 us (97%)
  local copies, waits for them, and re-layouts  1.41 us (2%)
    pallas_call x1, Pallas kernels, local_fused(): pl.pallas_call(fused, out_shape=(out, out), in_specs=[pl.BlockSpec(memory...  71.3 us

profile of v8, /device:TPU:0, one launch (start us, length us, event | category | flops | bytes accessed | tf_op | source)
XLA Modules:
  0.0 73.3 jit_solution(1582668948098875402)
XLA Ops:
  0.6 71.3 %shard_map.50 = (bf16[128,1024]{1,0:T(8,128)(2,1)S(1)}, bf16[128,1024]{1,0:T(8,128)(2,1)S(1)}) custom-call(bf16[128,1024]{1,0:T(8,128)(2,1)} %one_hbm.1, bf16[128,1024]{1,0:T(8,128)(2,1)} %two_hbm.1, bf16[4096,1024]{1,0:T(8,128)(2,1)} %weight_hbm.1), custom_call_target="tpu_custom_call" | custom-call | flops 3221225472 | bytes 9437184 | tf_op jit(solution)/shard_map/pallas_call | solution.py:432
  71.9 0.7 copy.7
  72.6 0.7 copy.8

commit v9 on v8

--- a/solution.py
+++ b/solution.py
@@ -10,7 +10,7 @@
 MESH = pl.DeviceIdType.MESH
 DP, MP = 8, 4
 VMEM_KIB = 54700
-PARTS = 4
+PARTS = 2
 
 
 def times_t(left, right):
@@ -61,7 +61,6 @@
     fetch[1].start()
     fetch[0].start()
     load = pltpu.make_async_copy(weight_hbm, weight, weight_sem)
-    load.start()
 
     barrier = pltpu.get_barrier_semaphore()
     for r in range(1, DP):
@@ -120,6 +119,7 @@
     for r in range(DP - 1, 0, -1):
         stat_copy(r).start()
     give_own(1)
+    load.start()
     for r in range(1, DP):
         stat_copy(r).wait_recv()
     for v in range(2):

time: 73.5 us -> 75.3 us (1.024)
  Pallas kernels: 71.3 us -> 73.1 us
    pallas_call x1, Pallas kernels: 71.3 us -> 73.1 us  [local_fused(): pl.pallas_call(fused, out_shape=(out, out), in_specs=[pl.BlockSpec(memory...]
where the time goes in v9:
time: 75.3 us; the launch traced here: 75.2 us
  Pallas kernels  73.1 us (97%)
  local copies, waits for them, and re-layouts  1.41 us (2%)
    pallas_call x1, Pallas kernels, local_fused(): pl.pallas_call(fused, out_shape=(out, out), in_specs=[pl.BlockSpec(memory...  73.1 us

profile of v9, /device:TPU:0, one launch (start us, length us, event | category | flops | bytes accessed | tf_op | source)
XLA Modules:
  0.0 75.2 jit_solution(8936403561738149859)
XLA Ops:
  0.6 73.1 %shard_map.50 = (bf16[128,1024]{1,0:T(8,128)(2,1)S(1)}, bf16[128,1024]{1,0:T(8,128)(2,1)S(1)}) custom-call(bf16[128,1024]{1,0:T(8,128)(2,1)} %one_hbm.1, bf16[128,1024]{1,0:T(8,128)(2,1)} %two_hbm.1, bf16[4096,1024]{1,0:T(8,128)(2,1)} %weight_hbm.1), custom_call_target="tpu_custom_call" | custom-call | flops 3221225472 | bytes 9437184 | tf_op jit(solution)/shard_map/pallas_call | solution.py:432
  73.8 0.7 copy.7
  74.5 0.7 copy.8

commit v10 on v8

--- a/solution.py
+++ b/solution.py
@@ -10,7 +10,7 @@
 MESH = pl.DeviceIdType.MESH
 DP, MP = 8, 4
 VMEM_KIB = 54700
-PARTS = 4
+PARTS = 8
 
 
 def times_t(left, right):

time: 73.5 us -> 74.1 us (level)
  no operation moved by 1% of the time
where the time goes in v10:
time: 74.1 us; the launch traced here: 74 us
  Pallas kernels  71.9 us (97%)
  local copies, waits for them, and re-layouts  1.41 us (2%)
    pallas_call x1, Pallas kernels, local_fused(): pl.pallas_call(fused, out_shape=(out, out), in_specs=[pl.BlockSpec(memory...  71.9 us

profile of v10, /device:TPU:0, one launch (start us, length us, event | category | flops | bytes accessed | tf_op | source)
XLA Modules:
  0.0 74.0 jit_solution(317664706823100899)
XLA Ops:
  0.6 71.9 %shard_map.50 = (bf16[128,1024]{1,0:T(8,128)(2,1)S(1)}, bf16[128,1024]{1,0:T(8,128)(2,1)S(1)}) custom-call(bf16[128,1024]{1,0:T(8,128)(2,1)} %one_hbm.1, bf16[128,1024]{1,0:T(8,128)(2,1)} %two_hbm.1, bf16[4096,1024]{1,0:T(8,128)(2,1)} %weight_hbm.1), custom_call_target="tpu_custom_call" | custom-call | flops 3221225472 | bytes 9437184 | tf_op jit(solution)/shard_map/pallas_call | solution.py:432
  72.6 0.7 copy.7
  73.3 0.7 copy.8
